TPU v7x, 32 devices: a whole 2x2x4 slice. The times are simulated.
32 devices in a mesh: dp: 2 (over core), ctx: 16 (over z, y, x).
Axes of the slice: x: 2, y: 2, z: 4, core: 2. Of those that a mesh axis runs over, the one named last changes fastest.
Arguments:
- queries: bfloat16 [4096, 1024], P(('dp', 'ctx')), parts along dimension 0, may hold values from -6 to 6
- keys: bfloat16 [4096, 256], P(('dp', 'ctx')), parts along dimension 0, may hold values from -6 to 6
- values: bfloat16 [4096, 256], P(('dp', 'ctx')), parts along dimension 0, may hold values from -6 to 6
- positions: int32 [4096], P(('dp', 'ctx')), parts along dimension 0, may hold values from 0 to 2047, as said below
Outputs:
- attended: bfloat16 [4096, 1024], P(('dp', 'ctx')), parts along dimension 0
- log_sum_exp: float32 [8, 4096], P(None, ('dp', 'ctx')), parts along dimension 1
There are 2 independent parts, one for each index of `dp`. A program takes and returns all parts, laid end to end along the dimension named above; each array names one. Nothing has to cross between parts.
Inputs may be any that keep to these rules, and one draw needn't show every extreme that they name: A permutation of the positions of one book; each index of ctx holds two runs of 64 consecutive positions, first run number c, then run number 2 * 16 - 1 - c, in units of 64 positions.
All inputs are finite; a program needn't handle non-finite values.
Results may differ from a plain program's by a relative error of at most 0.0055.
Values may be sent and summed in bfloat16 or wider, within the bound.
No kernel may reach another device: no remote copies, remote signals or barrier semaphores. Data moves between devices by JAX's collectives and lax.ppermute only.
A program may use at most 64 MiB of HBM per device.

v0:
```python
import jax
import jax.numpy as jnp
from jax import lax
from jax.sharding import PartitionSpec as P

HD = 128
QH = 8
KVH = 2


def attend(carry, grouped, block_keys, block_values, block_pos, query_pos):
    maxima, totals, accumulated = carry
    count_rows = block_keys.shape[0]
    key_heads = block_keys.reshape(count_rows, KVH, HD)
    value_heads = block_values.reshape(count_rows, KVH, HD)
    scores = jnp.einsum(
        "qhgd,khd->hgqk", grouped, key_heads, preferred_element_type=jnp.float32
    ) * HD ** (-0.5)
    allowed = jnp.logical_and(query_pos[:, None] >= block_pos[None, :], True)
    scores = jnp.where(allowed, scores, -1e30)
    newest = jnp.maximum(maxima, jnp.max(scores, axis=-1))
    weights = jnp.where(allowed, jnp.exp(scores - newest[..., None]), 0.0)
    shrink = jnp.exp(maxima - newest)
    totals = totals * shrink + jnp.sum(weights, axis=-1)
    update = jnp.einsum(
        "hgqk,khd->hgqd",
        weights.astype(jnp.bfloat16),
        value_heads,
        preferred_element_type=jnp.float32,
    )
    accumulated = accumulated * shrink[..., None] + update
    return (newest, totals, accumulated)


def fold_rows(carry, grouped, piece, query_pos):
    block_keys, block_values, block_pos = piece
    count_rows = block_keys.shape[0]
    splits = count_rows // 512
    stacked = (
        block_keys.reshape(splits, 512, block_keys.shape[1]),
        block_values.reshape(splits, 512, block_values.shape[1]),
        block_pos.reshape(splits, 512),
    )

    def inner(state, blocks):
        return (attend(state, grouped, blocks[0], blocks[1], blocks[2], query_pos), None)

    carry, unused_out = lax.scan(inner, carry, stacked)
    return carry


def shards(queries, keys, values, positions):
    rows = queries.shape[0]
    groups = QH // KVH
    grouped = queries.reshape(rows, KVH, groups, HD)
    initial = (
        jnp.full((KVH, groups, rows), -1e30, jnp.float32),
        jnp.zeros((KVH, groups, rows), jnp.float32),
        jnp.zeros((KVH, groups, rows, HD), jnp.float32),
    )
    state = fold_rows(
        initial,
        grouped,
        (
            lax.all_gather(keys, "ctx", axis=0, tiled=True),
            lax.all_gather(values, "ctx", axis=0, tiled=True),
            lax.all_gather(positions, "ctx", axis=0, tiled=True),
        ),
        positions,
    )
    maxima, totals, accumulated = state
    output = accumulated / totals[..., None]
    attended = jnp.transpose(output, (2, 0, 1, 3)).reshape(rows, QH * HD).astype(jnp.bfloat16)
    log_sum_exp = (maxima + jnp.log(totals)).reshape(QH, rows)
    return (attended, log_sum_exp)


def solution(mesh):
    return jax.shard_map(
        shards,
        mesh=mesh,
        in_specs=(
            P(("dp", "ctx"), None),
            P(("dp", "ctx"), None),
            P(("dp", "ctx"), None),
            P(("dp", "ctx")),
        ),
        out_specs=(P(("dp", "ctx"), None), P(None, ("dp", "ctx"))),
        check_vma=False,
    )
```

profile of v0, /device:TPU:0, one launch (start us, length us, event | category | flops | bytes accessed | tf_op | source)
XLA Modules:
  0.0 151.5 jit_solution(12555147820236022011)
XLA Ops:
  7.2 0.7 all-gather.4.cloned.1.call-update
  7.9 0.7 all-gather.6.cloned.1.call-update
  8.7 42.4 %all-gather = s32[16,1,128]{2,1,0:T(1,128)S(1)} all-gather(s32[1,1,128]{2,1,0:T(1,128)} %bitcast.61), channel_id=1, replica_groups=mesh['dp'=2,'ctx'=16] {'ctx'}, dimensions={0}, use_global_device_ids=true | all-gather | bytes 8704 | tf_op jit(solution)/shard_map/all_gather | solution.py:67
  51.0 0.5 broadcast.39
  51.6 0.7 reduce.3
  52.2 1.1 copy.25
  53.6 15.2 %all-gather.4.cloned.1.call-done = bf16[2048,256]{1,0:T(8,128)(2,1)} async-done(((bf16[128,256]{1,0:T(8,128)(2,1)}), bf16[2048,256]{1,0:T(8,128)(2,1)}) %all-gather.4.cloned.1.call-update) | async-done | bytes 1048592 | tf_op jit(solution)/shard_map/all_gather | solution.py:65
  68.8 56.9 %all-gather.6.cloned.1.call-done = bf16[2048,256]{1,0:T(8,128)(2,1)} async-done(((bf16[128,256]{1,0:T(8,128)(2,1)}), bf16[2048,256]{1,0:T(8,128)(2,1)}) %all-gather.6.cloned.1.call-update) | async-done | bytes 1048592 | tf_op jit(solution)/shard_map/all_gather | solution.py:66
  125.6 17.1 %while.15 = (s32[]{:T(128)}, f32[2,4,128]{2,1,0:T(4,128)S(1)}, f32[2,4,128]{2,1,0:T(4,128)S(1)}, f32[2,4,128,128]{3,2,1,0:T(8,128)S(1)}, s32[128]{0:T(128)}, /*i...) while((s32[]{:T(128)}, f32[2,4,128]{2,1,0:T(4,128)S(1)}, ...), condition=%wide.region_3.4_spmd.clone, body=%wide.region_0.3_spmd.clone.sunk | while | flops 275715072 | bytes 10558089 | solution.py:48
  125.6 0.8 broadcast_compare_fusion.2
  126.4 1.1 constant_dynamic-slice_fusion.6
  127.8 0.5 fusion.27
  128.4 0.5 fusion.28
  128.9 1.0 convolution_add_fusion.2
  129.9 0.8 broadcast_compare_fusion.2
  130.7 1.1 constant_dynamic-slice_fusion.6
  132.1 0.5 fusion.27
  132.6 0.5 fusion.28
  133.2 1.0 convolution_add_fusion.2
  134.2 0.8 broadcast_compare_fusion.2
  135.0 1.1 constant_dynamic-slice_fusion.6
  136.4 0.5 fusion.27
  136.9 0.5 fusion.28
  137.5 1.0 convolution_add_fusion.2
  138.5 0.8 broadcast_compare_fusion.2
  139.3 1.1 constant_dynamic-slice_fusion.6
  140.7 0.5 fusion.27
  141.2 0.5 fusion.28
  141.7 1.0 convolution_add_fusion.2
  142.7 0.2 fusion.12
  143.2 0.9 convert_element_type.14
  144.0 0.6 log_add_fusion
  (32 shorter events, 1.7 us)
Async XLA Ops:
  7.2 61.6 %all-gather.4.cloned.1.call-start = ((), (), s32[]{:S(2)}) async-start(), calls=%async_computation | async-start | bytes 1114112 | tf_op jit(solution)/shard_map/all_gather | solution.py:65
  7.9 117.7 %all-gather.6.cloned.1.call-start = ((), (), s32[]{:S(2)}) async-start(), calls=%async_computation.1 | async-start | bytes 1114112 | tf_op jit(solution)/shard_map/all_gather | solution.py:66
Sparse Core Ops, SparseCore 0:
  10.8 57.9 all-gather.3
  71.5 54.0 all-gather.5
where the time goes:
time: 152 us; the launch traced here: 151 us
  waiting for transfers between devices  73.5 us (48%)
  blocking collectives  42.4 us (28%)
  between operations  14.1 us (9%)
  local copies, waits for them, and re-layouts  8.35 us (5%)
  other arithmetic  6.82 us (4%)
  matrix products  6.04 us (4%)
    all_gather x1, waiting for transfers between devices, shards(): lax.all_gather(values, 'ctx', axis=0, tiled=True)  56.9 us
    all_gather x1, blocking collectives, shards(): lax.all_gather(positions, 'ctx', axis=0, tiled=True)  42.4 us
    all_gather x1, waiting for transfers between devices, shards(): lax.all_gather(keys, 'ctx', axis=0, tiled=True)  15.2 us
    dynamic_slice x16, local copies, waits for them, and re-layouts, fold_rows(): carry, unused_out = lax.scan(inner, carry, stacked)  5.44 us
    dot_general x4, matrix products, attend(): jnp.einsum('hgqk,khd->hgqd', weights.astype(jnp.bfloat16), value_heads, p...  3.88 us
    ge x4, other arithmetic, attend(): allowed = jnp.logical_and(query_pos[:, None] >= block_pos[None, :], True)  3.16 us
  transfers between devices with their start and end apart: 2, of which 2 were waited for; matrix products, arithmetic and copies ran while one was open for 2% of the time, Pallas kernels for 0%

commit v1 on v0

v1 whole, which is shorter than its diff:
```python
import functools
import math

import jax
import jax.numpy as jnp
from jax import lax
from jax.experimental import pallas as pl
from jax.experimental.pallas import tpu as pltpu
from jax.sharding import PartitionSpec as P

HD = 128
QH = 8
KVH = 2
GROUPS = QH // KVH
TAIL = 16
RUN = 64
MASKED = -1e30
LOWEST = -1e25
SCALE = HD ** (-0.5) * math.log2(math.e)
LN2 = math.log(2.0)
AXES = ("dp", "ctx")
VMEM = pl.BlockSpec(memory_space=pltpu.VMEM)


def call(kernel, outs, name, flops, count):
    return pl.pallas_call(
        kernel,
        out_shape=outs,
        in_specs=[VMEM] * count,
        out_specs=jax.tree.map(lambda unused: VMEM, outs),
        compiler_params=pltpu.CompilerParams(vmem_limit_bytes=32 * 1024 * 1024),
        cost_estimate=pl.CostEstimate(flops=flops, bytes_accessed=1 << 20, transcendentals=flops // 512),
        name=name,
    )


def position_rows(pos_ref):
    pos = pos_ref[...].reshape(1, -1)
    row = lax.broadcasted_iota(jnp.int32, (TAIL, pos.shape[1]), 0)
    high, low = lax.shift_right_logical(pos, 6), jnp.bitwise_and(pos, RUN - 1)
    return jnp.where(row == 0, high, jnp.where(row == 1, low, 0)).astype(jnp.float32).astype(jnp.bfloat16)


def pack_heads(heads, out_ref, source_ref, first):
    rows = source_ref.shape[0]
    for head in range(heads):
        out_ref[(first + head) * rows : (first + head + 1) * rows, :] = source_ref[:, head * HD : (head + 1) * HD]


def pack_kv_kernel(keys_ref, values_ref, pos_ref, out_ref):
    pack_heads(KVH, out_ref, keys_ref, 0)
    pack_heads(KVH, out_ref, values_ref, KVH)
    out_ref[out_ref.shape[0] - TAIL :, :] = position_rows(pos_ref)


def pack_q_kernel(queries_ref, pos_ref, out_ref):
    pack_heads(QH, out_ref, queries_ref, 0)
    out_ref[out_ref.shape[0] - TAIL :, :] = position_rows(pos_ref)


def positions_of(tail):
    tail = tail.astype(jnp.float32)
    return tail[0:1, :] * RUN + tail[1:2, :]


def column_of(row):
    return jnp.transpose(jnp.broadcast_to(row, (row.shape[1], row.shape[1])))


def absorb(queries, blocks, state, rows):
    query_pos = column_of(positions_of(queries[QH * rows :, :]))
    size = 2 * KVH * rows + TAIL
    allowed = []
    for ref, base in blocks:
        key_pos = positions_of(ref[base + size - TAIL : base + size, :])
        allowed.append(query_pos >= key_pos)
    for head in range(KVH):
        heads = queries[head * GROUPS * rows : (head + 1) * GROUPS * rows, :]
        scores = []
        for (ref, base), mask in zip(blocks, allowed):
            block_keys = ref[base + head * rows : base + (head + 1) * rows, :]
            part = lax.dot_general(heads, block_keys, (((1,), (1,)), ((), ())), preferred_element_type=jnp.float32)
            part = jnp.where(mask[None], part.reshape(GROUPS, rows, rows), MASKED)
            scores.append(part.reshape(GROUPS * rows, rows))
        top = functools.reduce(jnp.maximum, scores)
        top = jnp.max(top, axis=1, keepdims=True) * SCALE
        if state is None:
            peak = jnp.maximum(top, LOWEST)
        else:
            acc_ref, stat_ref = state
            old = jnp.concatenate([stat_ref[:, head * GROUPS + g : head * GROUPS + g + 1] for g in range(GROUPS)], axis=0)
            old_total = jnp.concatenate(
                [stat_ref[:, QH + head * GROUPS + g : QH + head * GROUPS + g + 1] for g in range(GROUPS)], axis=0
            )
            peak = jnp.maximum(top, old)
        sums = None
        accumulated = None
        for (ref, base), part in zip(blocks, scores):
            weights = jnp.exp2(part * SCALE - peak)
            sums = weights if sums is None else sums + weights
            block_values = ref[base + (KVH + head) * rows : base + (KVH + head + 1) * rows, :]
            update = jnp.dot(weights.astype(jnp.bfloat16), block_values, preferred_element_type=jnp.float32)
            accumulated = update if accumulated is None else accumulated + update
        total = jnp.sum(sums, axis=1, keepdims=True)
        if state is not None:
            shrink = jnp.exp2(old - peak)
            total = total + old_total * shrink
            accumulated = accumulated + acc_ref[head * GROUPS * rows : (head + 1) * GROUPS * rows, :] * shrink
        yield head, peak, total, accumulated


def lane_table(columns, rows):
    lane = lax.broadcasted_iota(jnp.int32, (rows, HD), 1)
    table = jnp.zeros((rows, HD), jnp.float32)
    for index, column in enumerate(columns):
        table = jnp.where(lane == index, column, table)
    return table


def write_state(results, acc_ref, stat_ref, rows):
    peaks, totals = [], []
    for head, peak, total, accumulated in results:
        acc_ref[head * GROUPS * rows : (head + 1) * GROUPS * rows, :] = accumulated
        for g in range(GROUPS):
            peaks.append(peak[g * rows : (g + 1) * rows, :])
            totals.append(total[g * rows : (g + 1) * rows, :])
    stat_ref[...] = lane_table(peaks + totals, rows)


def absorb_kernel(rows, bases, sides, fresh, *refs):
    queries, refs = refs[:sides], refs[sides:]
    states, refs = ([], refs) if fresh else (refs[: 2 * sides], refs[2 * sides :])
    arrays, outs = refs[: len(bases)], refs[len(bases) :]
    blocks = [(ref, base) for ref, several in zip(arrays, bases) for base in several]
    for side in range(sides):
        state = None if fresh else states[2 * side : 2 * side + 2]
        write_state(absorb(queries[side], blocks, state, rows), outs[2 * side], outs[2 * side + 1], rows)


def message_kernel(rows, bases, *refs):
    queries, acc_ref, stat_ref = refs[:3]
    arrays, out_ref = refs[3 : 3 + len(bases)], refs[3 + len(bases)]
    blocks = [(ref, base) for ref, several in zip(arrays, bases) for base in several]
    logs = []
    for head, peak, total, accumulated in absorb(queries, blocks, (acc_ref, stat_ref), rows):
        safe = jnp.maximum(total, 1e-30)
        out_ref[head * GROUPS * rows : (head + 1) * GROUPS * rows, :] = (accumulated / safe).astype(jnp.bfloat16)
        log = jnp.where(total > 0.0, peak + jnp.log2(safe), LOWEST)
        for g in range(GROUPS):
            logs.append(log[g * rows : (g + 1) * rows, :])
    rest = jnp.transpose(lane_table(logs, rows))[:QH, :]
    pieces = []
    for unused in range(3):
        piece = rest.astype(jnp.bfloat16)
        pieces.append(piece.astype(jnp.float32))
        rest = rest - pieces[-1]
    pieces.append(jnp.zeros_like(rest))
    out_ref[QH * rows :, :] = jnp.concatenate(pieces, axis=0).astype(jnp.bfloat16)


def merge_kernel(rows, acc_ref, stat_ref, message_ref, attended_ref, log_ref):
    tail = message_ref[QH * rows :, :].astype(jnp.float32)
    theirs_row = tail[:QH] + tail[QH : 2 * QH] + tail[2 * QH : 3 * QH]
    theirs = jnp.transpose(jnp.concatenate([theirs_row, jnp.zeros((HD - QH, rows), jnp.float32)], axis=0))
    stats = stat_ref[...]
    logs = []
    for head in range(QH):
        peak, total = stats[:, head : head + 1], stats[:, QH + head : QH + head + 1]
        their = theirs[:, head : head + 1]
        mine = peak + jnp.log2(total)
        top = jnp.maximum(mine, their)
        denominator = jnp.exp2(mine - top) + jnp.exp2(their - top)
        joint = top + jnp.log2(denominator)
        logs.append(joint * LN2)
        block = acc_ref[head * rows : (head + 1) * rows, :] * (jnp.exp2(peak - joint))
        other = message_ref[head * rows : (head + 1) * rows, :].astype(jnp.float32) * jnp.exp2(their - joint)
        attended_ref[:, head * HD : (head + 1) * HD] = (block + other).astype(jnp.bfloat16)
    log_ref[...] = jnp.transpose(lane_table(logs, rows))[:QH, :]


def shards(dp, ctx, queries, keys, values, positions):
    rows = queries.shape[0]
    size = 2 * KVH * rows + TAIL
    queries_size = QH * rows + TAIL
    message_size = QH * rows + 4 * QH
    flops = 4 * rows * rows * HD * QH
    f32, bf16 = jnp.float32, jnp.bfloat16
    state = (jax.ShapeDtypeStruct((QH * rows, HD), f32), jax.ShapeDtypeStruct((rows, HD), f32))

    def exchange(array, even, odd=None):
        masks = (even, even if odd is None else odd)
        pairs = [(d * ctx + i, d * ctx + (i ^ masks[d % 2])) for d in range(dp) for i in range(ctx)]
        return lax.ppermute(array, AXES, pairs)

    def several(arrays):
        return [tuple(range(0, array.shape[0], size)) for array in arrays]

    def absorb_call(name, sides, states, arrays):
        bases = several(arrays)
        count = sum(map(len, bases))
        kernel = functools.partial(absorb_kernel, rows, bases, len(sides), not states)
        inputs = list(sides) + list(states) + list(arrays)
        return call(kernel, list(state) * len(sides), name, flops * count * len(sides), len(inputs))(*inputs)

    kv = call(pack_kv_kernel, jax.ShapeDtypeStruct((size, HD), bf16), "pack_kv", 0, 3)(keys, values, positions)
    q = call(pack_q_kernel, jax.ShapeDtypeStruct((queries_size, HD), bf16), "pack_q", 0, 2)(queries, positions)
    if ctx == 16:
        far, near, side_even, side_odd = 12, 4, 1, 2
        z3 = exchange(kv, far)
        z1 = exchange(kv, near)
        theirs = exchange(q, side_even, side_odd)
        y0 = exchange(kv, side_odd, side_even)
        z2 = exchange(z3, near)
        y13 = exchange(jnp.concatenate([z1, z3]), side_odd, side_even)
        y2 = exchange(z2, side_odd, side_even)
        early, late = [[kv, y0, z1, z3]], [z2, y13, y2]
    else:
        theirs = exchange(q, 1)
        early, late = [[kv]], []
        held = [kv]
        bit = 2
        while bit < ctx:
            got = [exchange(block, bit) for block in held]
            held = held + got
            bit *= 2
        rest = held[1:]
        groups = [rest[i : i + 4] for i in range(0, len(rest), 4)]
        early, late = early + groups[:-1], groups[-1]
    states = []
    for group in early:
        states = absorb_call("absorb_early", (theirs, q), states, group)
    bases = several(late)
    count = sum(map(len, bases))
    message = call(
        functools.partial(message_kernel, rows, bases),
        jax.ShapeDtypeStruct((message_size, HD), bf16),
        "absorb_theirs",
        flops * count,
        3 + len(late),
    )(theirs, states[0], states[1], *late)
    other = exchange(message, 1, 2 if ctx == 16 else None)
    mine = absorb_call("absorb_mine", (q,), states[2:], late)
    outs = (jax.ShapeDtypeStruct((rows, QH * HD), bf16), jax.ShapeDtypeStruct((QH, rows), f32))
    return call(functools.partial(merge_kernel, rows), outs, "merge", 0, 3)(mine[0], mine[1], other)


def solution(mesh):
    return jax.shard_map(
        functools.partial(shards, mesh.shape["dp"], mesh.shape["ctx"]),
        mesh=mesh,
        in_specs=(
            P(("dp", "ctx"), None),
            P(("dp", "ctx"), None),
            P(("dp", "ctx"), None),
            P(("dp", "ctx")),
        ),
        out_specs=(P(("dp", "ctx"), None), P(None, ("dp", "ctx"))),
        check_vma=False,
    )
```

time: 152 us -> 37 us (0.24)
  waiting for transfers between devices: 73.5 us -> 12.7 us
  blocking collectives: 42.4 us -> 0 us
  between operations: 14.1 us -> 0.68 us
  starting transfers between devices: 0.08 us -> 13.3 us
  Pallas kernels: 0 us -> 7.82 us
  other arithmetic: 6.82 us -> 0.02 us
  matrix products: 6.04 us -> 0 us
  local copies, waits for them, and re-layouts: 8.35 us -> 2.33 us
    all_gather x2 -> x0, waiting for transfers between devices: 72.1 us -> none  [the longest x1 56.9 us: shards(): lax.all_gather(values, 'ctx', axis=0, tiled=True)]
    all_gather x1 -> x0, blocking collectives: 42.4 us -> none  [shards(): lax.all_gather(positions, 'ctx', axis=0, tiled=True)]
    ppermute x0 -> x8, starting transfers between devices: none -> 13.3 us  [exchange(): return lax.ppermute(array, AXES, pairs)]
    ppermute x0 -> x8, waiting for transfers between devices: none -> 12.7 us  [exchange(): return lax.ppermute(array, AXES, pairs)]
    pallas_call x0 -> x6, Pallas kernels: none -> 7.82 us  [the longest x2 3.76 us: absorb_call(): call(kernel, list(state) * len(sides), name, flops * count * len(sides),...]
    dot_general x8 -> x0, matrix products: 6.04 us -> none  [the longest x4 3.88 us: attend(): jnp.einsum('hgqk,khd->hgqd', weights.astype(jnp.bfloat16), value_heads, p...]
    dynamic_slice x16 -> x0, local copies, waits for them, and re-layouts: 5.44 us -> none  [fold_rows(): carry, unused_out = lax.scan(inner, carry, stacked)]
    ge x4 -> x0, other arithmetic: 3.16 us -> none  [attend(): allowed = jnp.logical_and(query_pos[:, None] >= block_pos[None, :], True)]
  transfers between devices with their start and end apart: 2 -> 8, of which waited for: 2 -> 6; matrix products, arithmetic and copies ran while one was open for 2% -> 0% of each run, Pallas kernels for 0% -> 10%
where the time goes in v1:
time: 37 us; the launch traced here: 36.8 us
  starting transfers between devices  13.3 us (36%)
  waiting for transfers between devices  12.7 us (34%)
  Pallas kernels  7.82 us (21%)
  local copies, waits for them, and re-layouts  2.33 us (6%)
  between operations  0.68 us (2%)
    ppermute x8, starting transfers between devices, exchange(): return lax.ppermute(array, AXES, pairs)  13.3 us
    ppermute x8, waiting for transfers between devices, exchange(): return lax.ppermute(array, AXES, pairs)  12.7 us
    pallas_call x2, Pallas kernels, absorb_call(): call(kernel, list(state) * len(sides), name, flops * count * len(sides),...  3.76 us
    pallas_call x1, Pallas kernels, shards(): call(functools.partial(message_kernel, rows, bases), jax.ShapeDtypeStruct...  2.66 us
    unnamed x8, local copies, waits for them, and re-layouts  2.33 us
    pallas_call x1, Pallas kernels, shards(): call(functools.partial(merge_kernel, rows), outs, 'merge', 0, 3)  1.33 us
  transfers between devices with their start and end apart: 8, of which 6 were waited for; matrix products, arithmetic and copies ran while one was open for 0% of the time, Pallas kernels for 10%

profile of v1, /device:TPU:0, one launch (start us, length us, event | category | flops | bytes accessed | tf_op | source)
XLA Modules:
  0.0 36.8 jit_solution(16302573463086961246)
XLA Ops:
  0.6 0.0 copy-start.1
  0.6 0.8 %copy-done.1 = bf16[128,256]{1,0:T(8,128)(2,1)S(1)} copy-done((bf16[128,256]{1,0:T(8,128)(2,1)S(1)}, bf16[128,256]{1,0:T(8,128)(2,1)}, u32[]{:S(2)}) %copy-start.1) | copy-done | bytes 65560
  1.5 0.0 copy-start.2
  1.5 0.8 %copy-done.2 = bf16[128,256]{1,0:T(8,128)(2,1)S(1)} copy-done((bf16[128,256]{1,0:T(8,128)(2,1)S(1)}, bf16[128,256]{1,0:T(8,128)(2,1)}, u32[]{:S(2)}) %copy-start.2) | copy-done | bytes 65560
  2.3 0.0 copy-start.3
  2.3 0.7 %copy-done.3 = s32[128]{0:T(128)S(1)} copy-done((s32[128]{0:T(128)S(1)}, s32[128]{0:T(128)}, u32[]{:S(2)}) %copy-start.3) | copy-done | bytes 536
  3.0 0.0 copy-start
  3.0 5.1 %collective-permute-start.3 = (bf16[528,128]{1,0:T(8,128)(2,1)S(1)}, bf16[528,128]{1,0:T(8,128)(2,1)S(1)}, u32[]{:S(2)}, u32[]{:S(2)}) collective-permute-start(bf16[528,128]{1,0:T(8,128)(2,1)S(1)} %pack_kv.1.refs_2_), channel_id=1, source_target_pairs={{0,12},{1,13},{2,14},{3,15},{4,8},{5,9},{6,10},{7,11},{8,4},{9,5},... | collective-permute-start | bytes 405512 | tf_op jit(solution)/shard_map/ppermute | solution.py:193
  8.1 0.0 collective-permute-start.2
  8.1 0.0 copy-done
  8.2 1.6 %collective-permute-start = (bf16[1040,128]{1,0:T(8,128)(2,1)S(1)}, bf16[1040,128]{1,0:T(8,128)(2,1)S(1)}, u32[]{:S(2)}, u32[]{:S(2)}) collective-permute-start(bf16[1040,128]{1,0:T(8,128)(2,1)S(1)} %pack_q.1.refs_1_.refs_0_), channel_id=1, source_target_pairs={{0,1},{1,0},{2,3},{3,2},{4,5},{5,4},{6,7},{7,6},{8,9},{9,8},{10,11... | collective-permute-start | bytes 798728 | tf_op jit(solution)/shard_map/ppermute | solution.py:193
  9.7 2.8 %collective-permute-done.3.refs_5_ = bf16[528,128]{1,0:T(8,128)(2,1)S(1)} collective-permute-done((bf16[528,128]{1,0:T(8,128)(2,1)S(1)}, bf16[528,128]{1,0:T(8,128)(2,1)S(1)}, u32[]{:S(2)}, u32[]{:S(2)}) %collective-permute-start.3) | collective-permute-done | bytes 135200 | tf_op jit(solution)/shard_map/ppermute | solution.py:193
  12.6 2.1 %collective-permute-done.2.refs_4_ = bf16[528,128]{1,0:T(8,128)(2,1)S(1)} collective-permute-done((bf16[528,128]{1,0:T(8,128)(2,1)S(1)}, bf16[528,128]{1,0:T(8,128)(2,1)S(1)}, u32[]{:S(2)}, u32[]{:S(2)}) %collective-permute-start.2) | collective-permute-done | bytes 135200 | tf_op jit(solution)/shard_map/ppermute | solution.py:193
  14.7 1.6 %collective-permute-start.5 = (bf16[1056,128]{1,0:T(8,128)(2,1)S(1)}, bf16[1056,128]{1,0:T(8,128)(2,1)S(1)}, u32[]{:S(2)}, u32[]{:S(2)}) collective-permute-start(bf16[1056,128]{1,0:T(8,128)(2,1)S(1)} %pad_maximum_fusion), channel_id=1, source_target_pairs={{0,2},{1,3},{2,0},{3,1},{4,6},{5,7},{6,4},{7,5},{8,10},{9,11},{10,... | collective-permute-start | bytes 811016 | tf_op jit(solution)/shard_map/ppermute | solution.py:193
  16.3 1.7 %collective-permute-start.4 = (bf16[528,128]{1,0:T(8,128)(2,1)S(1)}, bf16[528,128]{1,0:T(8,128)(2,1)S(1)}, u32[]{:S(2)}, u32[]{:S(2)}) collective-permute-start(bf16[528,128]{1,0:T(8,128)(2,1)S(1)} %collective-permute-done.3.refs_5_), channel_id=1, source_target_pairs={{0,4},{1,5},{2,6},{3,7},{4,0},{5,1},{6,2},{7,3},{8,12},{9,13},{10,... | collective-permute-start | bytes 405512 | tf_op jit(solution)/shard_map/ppermute | solution.py:193
  18.0 0.5 %collective-permute-start.1 = (bf16[528,128]{1,0:T(8,128)(2,1)S(1)}, bf16[528,128]{1,0:T(8,128)(2,1)S(1)}, u32[]{:S(2)}, u32[]{:S(2)}) collective-permute-start(bf16[528,128]{1,0:T(8,128)(2,1)S(1)} %pack_kv.1.refs_2_), channel_id=1, source_target_pairs={{0,2},{1,3},{2,0},{3,1},{4,6},{5,7},{6,4},{7,5},{8,10},{9,11},{10,... | collective-permute-start | bytes 405512 | tf_op jit(solution)/shard_map/ppermute | solution.py:193
  18.5 2.8 %collective-permute-done.4.refs_3_ = bf16[528,128]{1,0:T(8,128)(2,1)S(1)} collective-permute-done((bf16[528,128]{1,0:T(8,128)(2,1)S(1)}, bf16[528,128]{1,0:T(8,128)(2,1)S(1)}, u32[]{:S(2)}, u32[]{:S(2)}) %collective-permute-start.4) | collective-permute-done | bytes 135200 | tf_op jit(solution)/shard_map/ppermute | solution.py:193
  21.3 1.3 %collective-permute-start.6 = (bf16[528,128]{1,0:T(8,128)(2,1)S(1)}, bf16[528,128]{1,0:T(8,128)(2,1)S(1)}, u32[]{:S(2)}, u32[]{:S(2)}) collective-permute-start(bf16[528,128]{1,0:T(8,128)(2,1)S(1)} %collective-permute-done.4.refs_3_), channel_id=1, source_target_pairs={{0,2},{1,3},{2,0},{3,1},{4,6},{5,7},{6,4},{7,5},{8,10},{9,11},{10,... | collective-permute-start | bytes 405512 | tf_op jit(solution)/shard_map/ppermute | solution.py:193
  22.6 0.4 collective-permute-done.1.refs_3_
  23.0 0.0 collective-permute-done.refs_0_
  23.0 2.2 %absorb_early.1 = (f32[1024,128]{1,0:T(8,128)S(1)}, f32[128,128]{1,0:T(8,128)S(1)}, f32[1024,128]{1,0:T(8,128)S(1)}, f32[128,128]{1,0:T(8,128)S(1)}) custom-call(bf16[1040,128]{1,0:T(8,128)(2,1)S(1)} %collective-permute-done.refs_0_, bf16[1040,128]{1,0:T(8,128)(2,1)S(1)} %pack_q.1.refs_1_.refs_0_, bf16[528,128]{1,0:T(8,128)(2,1)S(1)} %pack_kv.1.refs_2_, ...), custom_call_target="tpu_custom_call" | custom-call | flops 536870912 | bytes 1048576 | tf_op jit(solution)/shard_map/absorb_early/pallas_call | solution.py:203
  25.2 0.0 collective-permute-done.5.refs_4_
  25.2 1.1 %collective-permute-done.6.refs_5_ = bf16[528,128]{1,0:T(8,128)(2,1)S(1)} collective-permute-done((bf16[528,128]{1,0:T(8,128)(2,1)S(1)}, bf16[528,128]{1,0:T(8,128)(2,1)S(1)}, u32[]{:S(2)}, u32[]{:S(2)}) %collective-permute-start.6) | collective-permute-done | bytes 135200 | tf_op jit(solution)/shard_map/ppermute | solution.py:193
  26.3 2.7 %absorb_theirs.1 = bf16[1056,128]{1,0:T(8,128)(2,1)S(1)} custom-call(bf16[1040,128]{1,0:T(8,128)(2,1)S(1)} %collective-permute-done.refs_0_, f32[1024,128]{1,0:T(8,128)S(1)} %get-tuple-element.12.refs_1_, f32[128,128]{1,0:T(8,128)S(1)} %get-tuple-element.13.refs_2_, bf16[528,128]{1,0:T(8,128)(2,1)S(1)} %collective-permute-done.4.refs_3_, ...), custom_call_target="tpu_custom_call" | custom-call | flops 268435456 | bytes 1048576 | tf_op jit(solution)/shard_map/absorb_theirs/pallas_call | solution.py:234
  29.0 1.5 %collective-permute-start.7 = (bf16[1056,128]{1,0:T(8,128)(2,1)S(1)}, bf16[1056,128]{1,0:T(8,128)(2,1)S(1)}, u32[]{:S(2)}, u32[]{:S(2)}) collective-permute-start(bf16[1056,128]{1,0:T(8,128)(2,1)S(1)} %absorb_theirs.1), channel_id=1, source_target_pairs={{0,1},{1,0},{2,3},{3,2},{4,5},{5,4},{6,7},{7,6},{8,9},{9,8},{10,11... | collective-permute-start | bytes 811016 | tf_op jit(solution)/shard_map/ppermute | solution.py:193
  30.5 1.6 %absorb_mine.1 = (f32[1024,128]{1,0:T(8,128)S(1)}, f32[128,128]{1,0:T(8,128)S(1)}) custom-call(bf16[1040,128]{1,0:T(8,128)(2,1)S(1)} %pack_q.1.refs_1_.refs_0_, f32[1024,128]{1,0:T(8,128)S(1)} %get-tuple-element.8.refs_1_, f32[128,128]{1,0:T(8,128)S(1)} %get-tuple-element.9.refs_2_, bf16[528,128]{1,0:T(8,128)(2,1)S(1)} %collective-permute-done.4.refs_3_, ...), custom_call_target="tpu_custom_call" | custom-call | flops 268435456 | bytes 1048576 | tf_op jit(solution)/shard_map/absorb_mine/pallas_call | solution.py:203
  32.1 3.4 %collective-permute-done.7.message_ref = bf16[1056,128]{1,0:T(8,128)(2,1)S(1)} collective-permute-done((bf16[1056,128]{1,0:T(8,128)(2,1)S(1)}, bf16[1056,128]{1,0:T(8,128)(2,1)S(1)}, u32[]{:S(2)}, u32[]{:S(2)}) %collective-permute-start.7) | collective-permute-done | bytes 270368 | tf_op jit(solution)/shard_map/ppermute | solution.py:193
  35.5 1.3 %merge.1 = (bf16[128,1024]{1,0:T(8,128)(2,1)}, f32[8,128]{1,0:T(8,128)}) custom-call(f32[1024,128]{1,0:T(8,128)S(1)} %get-tuple-element.10.acc_ref, f32[128,128]{1,0:T(8,128)S(1)} %get-tuple-element.11.stat_ref, bf16[1056,128]{1,0:T(8,128)(2,1)S(1)} %collective-permute-done.7.message_ref), custom_call_target="tpu_custom_call" | custom-call | bytes 1048576 | tf_op jit(solution)/shard_map/merge/pallas_call | solution.py:244
  (3 shorter events, 0.1 us)
Async XLA Ops:
  0.6 0.8 %copy-start.1 = (bf16[128,256]{1,0:T(8,128)(2,1)S(1)}, bf16[128,256]{1,0:T(8,128)(2,1)}, u32[]{:S(2)}) copy-start(bf16[128,256]{1,0:T(8,128)(2,1)} %keys_ref.1) | copy-start | bytes 196612
  1.5 0.8 %copy-start.2 = (bf16[128,256]{1,0:T(8,128)(2,1)S(1)}, bf16[128,256]{1,0:T(8,128)(2,1)}, u32[]{:S(2)}) copy-start(bf16[128,256]{1,0:T(8,128)(2,1)} %values_ref.1) | copy-start | bytes 196612
  2.3 0.7 %copy-start.3 = (s32[128]{0:T(128)S(1)}, s32[128]{0:T(128)}, u32[]{:S(2)}) copy-start(s32[128]{0:T(128)} %pos_ref.3) | copy-start | bytes 1540
  3.0 5.2 %copy-start = (bf16[128,1024]{1,0:T(8,128)(2,1)S(1)}, bf16[128,1024]{1,0:T(8,128)(2,1)}, u32[]{:S(2)}) copy-start(bf16[128,1024]{1,0:T(8,128)(2,1)} %queries_ref.1) | copy-start | bytes 786436
  3.0 9.6 %collective-permute-start.3 = (bf16[528,128]{1,0:T(8,128)(2,1)S(1)}, bf16[528,128]{1,0:T(8,128)(2,1)S(1)}, u32[]{:S(2)}, u32[]{:S(2)}) collective-permute-start(bf16[528,128]{1,0:T(8,128)(2,1)S(1)} %pack_kv.1.refs_2_), channel_id=1, source_target_pairs={{0,12},{1,13},{2,14},{3,15},{4,8},{5,9},{6,10},{7,11},{8,4},{9,5},... | collective-permute-start | bytes 405512 | tf_op jit(solution)/shard_map/ppermute | solution.py:193
  8.1 6.6 %collective-permute-start.2 = (bf16[528,128]{1,0:T(8,128)(2,1)S(1)}, bf16[528,128]{1,0:T(8,128)(2,1)S(1)}, u32[]{:S(2)}, u32[]{:S(2)}) collective-permute-start(bf16[528,128]{1,0:T(8,128)(2,1)S(1)} %pack_kv.1.refs_2_), channel_id=1, source_target_pairs={{0,4},{1,5},{2,6},{3,7},{4,0},{5,1},{6,2},{7,3},{8,12},{9,13},{10,... | collective-permute-start | bytes 405512 | tf_op jit(solution)/shard_map/ppermute | solution.py:193
  8.2 14.8 %collective-permute-start = (bf16[1040,128]{1,0:T(8,128)(2,1)S(1)}, bf16[1040,128]{1,0:T(8,128)(2,1)S(1)}, u32[]{:S(2)}, u32[]{:S(2)}) collective-permute-start(bf16[1040,128]{1,0:T(8,128)(2,1)S(1)} %pack_q.1.refs_1_.refs_0_), channel_id=1, source_target_pairs={{0,1},{1,0},{2,3},{3,2},{4,5},{5,4},{6,7},{7,6},{8,9},{9,8},{10,11... | collective-permute-start | bytes 798728 | tf_op jit(solution)/shard_map/ppermute | solution.py:193
  14.7 10.5 %collective-permute-start.5 = (bf16[1056,128]{1,0:T(8,128)(2,1)S(1)}, bf16[1056,128]{1,0:T(8,128)(2,1)S(1)}, u32[]{:S(2)}, u32[]{:S(2)}) collective-permute-start(bf16[1056,128]{1,0:T(8,128)(2,1)S(1)} %pad_maximum_fusion), channel_id=1, source_target_pairs={{0,2},{1,3},{2,0},{3,1},{4,6},{5,7},{6,4},{7,5},{8,10},{9,11},{10,... | collective-permute-start | bytes 811016 | tf_op jit(solution)/shard_map/ppermute | solution.py:193
  16.3 5.0 %collective-permute-start.4 = (bf16[528,128]{1,0:T(8,128)(2,1)S(1)}, bf16[528,128]{1,0:T(8,128)(2,1)S(1)}, u32[]{:S(2)}, u32[]{:S(2)}) collective-permute-start(bf16[528,128]{1,0:T(8,128)(2,1)S(1)} %collective-permute-done.3.refs_5_), channel_id=1, source_target_pairs={{0,4},{1,5},{2,6},{3,7},{4,0},{5,1},{6,2},{7,3},{8,12},{9,13},{10,... | collective-permute-start | bytes 405512 | tf_op jit(solution)/shard_map/ppermute | solution.py:193
  18.0 5.0 %collective-permute-start.1 = (bf16[528,128]{1,0:T(8,128)(2,1)S(1)}, bf16[528,128]{1,0:T(8,128)(2,1)S(1)}, u32[]{:S(2)}, u32[]{:S(2)}) collective-permute-start(bf16[528,128]{1,0:T(8,128)(2,1)S(1)} %pack_kv.1.refs_2_), channel_id=1, source_target_pairs={{0,2},{1,3},{2,0},{3,1},{4,6},{5,7},{6,4},{7,5},{8,10},{9,11},{10,... | collective-permute-start | bytes 405512 | tf_op jit(solution)/shard_map/ppermute | solution.py:193
  21.3 5.0 %collective-permute-start.6 = (bf16[528,128]{1,0:T(8,128)(2,1)S(1)}, bf16[528,128]{1,0:T(8,128)(2,1)S(1)}, u32[]{:S(2)}, u32[]{:S(2)}) collective-permute-start(bf16[528,128]{1,0:T(8,128)(2,1)S(1)} %collective-permute-done.4.refs_3_), channel_id=1, source_target_pairs={{0,2},{1,3},{2,0},{3,1},{4,6},{5,7},{6,4},{7,5},{8,10},{9,11},{10,... | collective-permute-start | bytes 405512 | tf_op jit(solution)/shard_map/ppermute | solution.py:193
  29.0 6.5 %collective-permute-start.7 = (bf16[1056,128]{1,0:T(8,128)(2,1)S(1)}, bf16[1056,128]{1,0:T(8,128)(2,1)S(1)}, u32[]{:S(2)}, u32[]{:S(2)}) collective-permute-start(bf16[1056,128]{1,0:T(8,128)(2,1)S(1)} %absorb_theirs.1), channel_id=1, source_target_pairs={{0,1},{1,0},{2,3},{3,2},{4,5},{5,4},{6,7},{7,6},{8,9},{9,8},{10,11... | collective-permute-start | bytes 811016 | tf_op jit(solution)/shard_map/ppermute | solution.py:193

commit v2 on v1

v2 whole, which is shorter than its diff:
```python
import functools
import math

import jax
import jax.numpy as jnp
from jax import lax
from jax.experimental import pallas as pl
from jax.experimental.pallas import tpu as pltpu
from jax.sharding import PartitionSpec as P

HD = 128
QH = 8
KVH = 2
GROUPS = QH // KVH
TAIL = 16
RUN = 64
MASKED = -1e30
LOWEST = -1e25
SCALE = HD ** (-0.5) * math.log2(math.e)
LN2 = math.log(2.0)
WIDTH = 2
AXES = ("dp", "ctx")
VMEM = pl.BlockSpec(memory_space=pltpu.VMEM)


def call(kernel, outs, name, flops, count):
    return pl.pallas_call(
        kernel,
        out_shape=outs,
        in_specs=[VMEM] * count,
        out_specs=jax.tree.map(lambda unused: VMEM, outs),
        compiler_params=pltpu.CompilerParams(vmem_limit_bytes=32 * 1024 * 1024),
        cost_estimate=pl.CostEstimate(flops=flops, bytes_accessed=1 << 20, transcendentals=flops // 512),
        name=name,
    )


def position_rows(pos_ref):
    pos = pos_ref[...].reshape(1, -1)
    row = lax.broadcasted_iota(jnp.int32, (TAIL, pos.shape[1]), 0)
    high, low = lax.shift_right_logical(pos, 6), jnp.bitwise_and(pos, RUN - 1)
    return jnp.where(row == 0, high, jnp.where(row == 1, low, 0)).astype(jnp.float32).astype(jnp.bfloat16)


def pack_kernel(turned, *refs):
    sources, pos_hbm, out_ref, pos_ref, held_ref, sems = refs[: len(turned)], *refs[len(turned) :]
    rows = pos_hbm.shape[0]
    copies = [pltpu.make_async_copy(pos_hbm, pos_ref, sems.at[0])]
    moves = []
    for source, (count, turn) in zip(sources, turned):
        for head in range(count):
            index = len(copies) - 1
            place = pl.ds(index * rows, rows)
            target = held_ref if turn else out_ref
            copies.append(
                pltpu.make_async_copy(source.at[:, pl.ds(head * HD, HD)], target.at[place, :], sems.at[index + 1])
            )
            moves.append(place if turn else None)
    for copy in copies:
        copy.start()
    copies[0].wait()
    out_ref[out_ref.shape[0] - TAIL :, :] = position_rows(pos_ref)
    for copy, place in zip(copies[1:], moves):
        copy.wait()
        if place is not None:
            out_ref[place, :] = held_ref[place, :].T


def pack(name, sources, turned, positions):
    rows = positions.shape[0]
    count = sum(heads for heads, unused in turned)
    return pl.pallas_call(
        functools.partial(pack_kernel, turned),
        out_shape=jax.ShapeDtypeStruct((count * rows + TAIL, HD), jnp.bfloat16),
        in_specs=[pl.BlockSpec(memory_space=pltpu.HBM)] * (len(sources) + 1),
        out_specs=VMEM,
        scratch_shapes=[
            pltpu.VMEM((rows,), jnp.int32),
            pltpu.VMEM((count * rows, HD), jnp.bfloat16),
            pltpu.SemaphoreType.DMA((count + 1,)),
        ],
        compiler_params=pltpu.CompilerParams(vmem_limit_bytes=32 * 1024 * 1024),
        cost_estimate=pl.CostEstimate(flops=0, bytes_accessed=count * rows * HD * 4, transcendentals=0),
        name=name,
    )(*[pltpu.with_memory_space_constraint(array, pltpu.HBM) for array in (*sources, positions)])


def pack_queries_kernel(queries_ref, message_ref, out_ref):
    rows = queries_ref.shape[0]
    out_ref[QH * rows :, :] = message_ref[2 * KVH * rows :, :]
    for head in range(QH):
        out_ref[head * rows : (head + 1) * rows, :] = queries_ref[:, head * HD : (head + 1) * HD].T


def positions_of(tail):
    tail = tail.astype(jnp.float32)
    return tail[0:1, :] * RUN + tail[1:2, :]


def column_of(row):
    return jnp.transpose(jnp.broadcast_to(row, (row.shape[1], row.shape[1])))


def masks_of(queries, blocks, rows):
    query_pos = positions_of(queries[QH * rows :, :])
    size = 2 * KVH * rows + TAIL
    return [query_pos >= column_of(positions_of(ref[base + size - TAIL : base + size, :])) for ref, base in blocks]


def absorb(queries, blocks, state, rows):
    allowed = masks_of(queries, blocks, rows)
    wide = [jnp.concatenate([mask] * WIDTH, axis=1) for mask in allowed]
    for head in range(0, QH, WIDTH):
        group = head // GROUPS
        heads = jnp.concatenate([queries[(head + g) * rows : (head + g + 1) * rows, :] for g in range(WIDTH)], axis=1)
        lanes = slice(head * rows, (head + WIDTH) * rows)
        scores = []
        for (ref, base), mask in zip(blocks, wide):
            block_keys = ref[base + group * rows : base + (group + 1) * rows, :]
            part = jnp.dot(block_keys, heads, preferred_element_type=jnp.float32)
            scores.append(jnp.where(mask, part, MASKED))
        top = functools.reduce(jnp.maximum, scores)
        peak = jnp.max(top, axis=0, keepdims=True) * SCALE
        if state is None:
            peak = jnp.maximum(peak, LOWEST)
        else:
            acc_ref, stat_ref = state
            old = stat_ref[0:1, lanes]
            peak = jnp.maximum(peak, old)
        sums = None
        accumulated = None
        for (ref, base), part in zip(blocks, scores):
            weights = jnp.exp2(part * SCALE - peak)
            sums = weights if sums is None else sums + weights
            block_values = ref[base + (KVH + group) * rows : base + (KVH + group + 1) * rows, :]
            update = jnp.dot(block_values, weights.astype(jnp.bfloat16), preferred_element_type=jnp.float32)
            accumulated = update if accumulated is None else accumulated + update
        total = jnp.sum(sums, axis=0, keepdims=True)
        if state is not None:
            shrink = jnp.exp2(old - peak)
            total = total + stat_ref[1:2, lanes] * shrink
            accumulated = accumulated + acc_ref[:, lanes] * shrink
        yield head, peak, total, accumulated


def absorb_kernel(rows, bases, sides, fresh, *refs):
    queries, refs = refs[:sides], refs[sides:]
    states, refs = ([], refs) if fresh else (refs[: 2 * sides], refs[2 * sides :])
    arrays, outs = refs[: len(bases)], refs[len(bases) :]
    blocks = [(ref, base) for ref, several in zip(arrays, bases) for base in several]
    for side in range(sides):
        state = None if fresh else states[2 * side : 2 * side + 2]
        acc_ref, stat_ref = outs[2 * side : 2 * side + 2]
        for head, peak, total, accumulated in absorb(queries[side], blocks, state, rows):
            lanes = slice(head * rows, (head + WIDTH) * rows)
            acc_ref[:, lanes] = accumulated
            stat_ref[0:1, lanes] = peak
            stat_ref[1:2, lanes] = total


def message_kernel(rows, bases, *refs):
    queries, acc_ref, stat_ref = refs[:3]
    arrays, out_ref = refs[3 : 3 + len(bases)], refs[3 + len(bases)]
    blocks = [(ref, base) for ref, several in zip(arrays, bases) for base in several]
    logs = []
    for head, peak, total, accumulated in absorb(queries, blocks, (acc_ref, stat_ref), rows):
        safe = jnp.maximum(total, 1e-30)
        output = (accumulated * (1.0 / safe)).astype(jnp.bfloat16)
        log = jnp.where(total > 0.0, peak + jnp.log2(safe), LOWEST)
        for g in range(WIDTH):
            out_ref[(head + g) * rows : (head + g + 1) * rows, :] = output[:, g * rows : (g + 1) * rows]
            logs.append(log[:, g * rows : (g + 1) * rows])
    rest = jnp.concatenate(logs, axis=0)
    pieces = []
    for unused in range(3):
        piece = rest.astype(jnp.bfloat16).astype(jnp.float32)
        pieces.append(piece)
        rest = rest - piece
    pieces.append(jnp.zeros_like(rest))
    out_ref[QH * rows :, :] = jnp.concatenate(pieces, axis=0).astype(jnp.bfloat16)


def finish_kernel(rows, acc_ref, stat_ref, message_ref, attended_ref, log_ref):
    tail = message_ref[QH * rows :, :].astype(jnp.float32)
    theirs = tail[:QH] + tail[QH : 2 * QH] + tail[2 * QH : 3 * QH]
    for head in range(QH):
        lanes = slice(head * rows, (head + 1) * rows)
        peak, total = stat_ref[0:1, lanes], stat_ref[1:2, lanes]
        their = theirs[head : head + 1, :]
        mine = peak + jnp.log2(total)
        top = jnp.maximum(mine, their)
        joint = top + jnp.log2(jnp.exp2(mine - top) + jnp.exp2(their - top))
        log_ref[head : head + 1, :] = joint * LN2
        block = acc_ref[:, lanes] * jnp.exp2(peak - joint)
        other = message_ref[lanes, :].astype(jnp.float32) * jnp.exp2(their - joint)
        attended_ref[:, head * HD : (head + 1) * HD] = (block + other).T.astype(jnp.bfloat16)


def shards(dp, ctx, queries, keys, values, positions):
    rows = queries.shape[0]
    size = 2 * KVH * rows + TAIL
    flops = 4 * rows * rows * HD * QH
    f32, bf16 = jnp.float32, jnp.bfloat16
    state = (jax.ShapeDtypeStruct((HD, QH * rows), f32), jax.ShapeDtypeStruct((2, QH * rows), f32))

    def exchange(array, even, odd=None):
        masks = (even, even if odd is None else odd)
        pairs = [(d * ctx + i, d * ctx + (i ^ masks[d % 2])) for d in range(dp) for i in range(ctx)]
        return lax.ppermute(array, AXES, pairs)

    def several(arrays):
        return [tuple(range(0, array.shape[0], size)) for array in arrays]

    def absorb_call(name, query, state_of, arrays, after=()):
        bases = several(arrays) + [()] * len(after)
        kernel = functools.partial(absorb_kernel, rows, bases, 1, not state_of)
        inputs = [query, *state_of, *arrays, *after]
        return call(kernel, list(state), name, flops * sum(map(len, bases)), len(inputs))(*inputs)

    kv = pack("pack_keys_values", (keys, values), ((KVH, False), (KVH, True)), positions)
    q = call(pack_queries_kernel, jax.ShapeDtypeStruct((QH * rows + TAIL, HD), bf16), "pack_queries", 0, 2)(queries, kv)
    if ctx == 16:
        near, far, side, other_side = 4, 12, (1, 2), (2, 1)
        z3 = exchange(kv, far)
        z1 = exchange(kv, near)
        y0 = exchange(kv, *other_side)
        theirs = exchange(q, *side)
        y3 = exchange(z3, *other_side)
        y2 = exchange(z3, *[mask ^ near for mask in other_side])
        z2 = exchange(z3, near)
        y1 = exchange(z1, *other_side)
        groups = [[kv, y0, z1, z3], [y3, y1, z2], [y2]]
        after = (y3,)
        mine_groups = [[kv, y0, z1, z3, z2, y1, y3, y2]]
    else:
        side, after = (1, 1), ()
        theirs = exchange(q, *side)
        held = [kv]
        bit = 2
        while bit < ctx:
            held = held + [exchange(block, bit) for block in held]
            bit *= 2
        groups = mine_groups = [held[i : i + 4] for i in range(0, len(held), 4)]
    partial = []
    for index, group in enumerate(groups[:-1]):
        partial = absorb_call("absorb_theirs", theirs, partial, group, () if index else after)
    late = groups[-1]
    message = call(
        functools.partial(message_kernel, rows, several(late)),
        jax.ShapeDtypeStruct((QH * rows + 4 * QH, HD), bf16),
        "message",
        flops * sum(map(len, several(late))),
        3 + len(late),
    )(theirs, *partial, *late)
    other = exchange(message, *side)
    mine = []
    for group in mine_groups:
        mine = absorb_call("absorb_mine", q, mine, group)
    outs = (jax.ShapeDtypeStruct((rows, QH * HD), bf16), jax.ShapeDtypeStruct((QH, rows), f32))
    return call(functools.partial(finish_kernel, rows), outs, "finish", 0, 3)(*mine, other)


def solution(mesh):
    return jax.shard_map(
        functools.partial(shards, mesh.shape["dp"], mesh.shape["ctx"]),
        mesh=mesh,
        in_specs=(
            P(("dp", "ctx"), None),
            P(("dp", "ctx"), None),
            P(("dp", "ctx"), None),
            P(("dp", "ctx")),
        ),
        out_specs=(P(("dp", "ctx"), None), P(None, ("dp", "ctx"))),
        check_vma=False,
    )
```

time: 37 us -> 29 us (0.78)
  waiting for transfers between devices: 12.7 us -> 6.28 us
  local copies, waits for them, and re-layouts: 2.33 us -> 0.01 us
  starting transfers between devices: 13.3 us -> 15 us
  Pallas kernels: 7.82 us -> 6.9 us
    ppermute x8 -> x9, waiting for transfers between devices: 12.7 us -> 6.28 us  [exchange(): return lax.ppermute(array, AXES, pairs)]
    unnamed x8 -> x2, local copies, waits for them, and re-layouts: 2.33 us -> 0.01 us
    ppermute x8 -> x9, starting transfers between devices: 13.3 us -> 15 us  [exchange(): return lax.ppermute(array, AXES, pairs)]
    pallas_call x6 -> x7, Pallas kernels: 7.82 us -> 6.9 us  [the longest x3 4.36 us: absorb_call(): call(kernel, list(state), name, flops * sum(map(len, bases)), len(inputs))]
  transfers between devices with their start and end apart: 8 -> 9, of which waited for: 6 -> 5; matrix products, arithmetic and copies ran while one was open for 0% -> 0% of each run, Pallas kernels for 10% -> 16%
where the time goes in v2:
time: 29 us; the launch traced here: 28.9 us
  starting transfers between devices  15 us (52%)
  Pallas kernels  6.9 us (24%)
  waiting for transfers between devices  6.28 us (22%)
  between operations  0.69 us (2%)
    ppermute x9, starting transfers between devices, exchange(): return lax.ppermute(array, AXES, pairs)  15 us
    ppermute x9, waiting for transfers between devices, exchange(): return lax.ppermute(array, AXES, pairs)  6.28 us
    pallas_call x3, Pallas kernels, absorb_call(): call(kernel, list(state), name, flops * sum(map(len, bases)), len(inputs))  4.36 us
    pallas_call x1, Pallas kernels, pack(): pl.pallas_call(functools.partial(pack_kernel, turned), out_shape=jax.Shap...  1.03 us
    pallas_call x1, Pallas kernels, shards(): call(functools.partial(finish_kernel, rows), outs, 'finish', 0, 3)  0.91 us
  transfers between devices with their start and end apart: 9, of which 5 were waited for; matrix products, arithmetic and copies ran while one was open for 0% of the time, Pallas kernels for 16%

profile of v2, /device:TPU:0, one launch (start us, length us, event | category | flops | bytes accessed | tf_op | source)
XLA Modules:
  0.0 28.9 jit_solution(1605204368050888830)
XLA Ops:
  0.6 0.0 copy-start
  0.6 1.0 %pack_keys_values.1.message_ref.refs_1_ = bf16[528,128]{1,0:T(8,128)(2,1)S(1)} custom-call(bf16[128,256]{1,0:T(8,128)(2,1)} %refs_0_.1, bf16[128,256]{1,0:T(8,128)(2,1)} %refs_1_.1, s32[128]{0:T(128)} %refs_2_.1), custom_call_target="tpu_custom_call" | custom-call | bytes 262144 | tf_op jit(solution)/shard_map/pack_keys_values/pallas_call | solution.py:72
  1.7 5.1 %collective-permute-start.2 = (bf16[528,128]{1,0:T(8,128)(2,1)S(1)}, bf16[528,128]{1,0:T(8,128)(2,1)S(1)}, u32[]{:S(2)}, u32[]{:S(2)}) collective-permute-start(bf16[528,128]{1,0:T(8,128)(2,1)S(1)} %pack_keys_values.1.message_ref.refs_1_), channel_id=1, source_target_pairs={{0,12},{1,13},{2,14},{3,15},{4,8},{5,9},{6,10},{7,11},{8,4},{9,5},... | collective-permute-start | bytes 405512 | tf_op jit(solution)/shard_map/ppermute | solution.py:209
  6.8 0.0 copy-done
  6.8 0.1 pack_queries.1.refs_0_
  6.9 1.6 %collective-permute-start.7 = (bf16[1040,128]{1,0:T(8,128)(2,1)S(1)}, bf16[1040,128]{1,0:T(8,128)(2,1)S(1)}, u32[]{:S(2)}, u32[]{:S(2)}) collective-permute-start(bf16[1040,128]{1,0:T(8,128)(2,1)S(1)} %pack_queries.1.refs_0_), channel_id=1, source_target_pairs={{0,1},{1,0},{2,3},{3,2},{4,5},{5,4},{6,7},{7,6},{8,9},{9,8},{10,11... | collective-permute-start | bytes 798728 | tf_op jit(solution)/shard_map/ppermute | solution.py:209
  8.5 0.0 collective-permute-start.1
  8.5 1.5 %collective-permute-start = (bf16[528,128]{1,0:T(8,128)(2,1)S(1)}, bf16[528,128]{1,0:T(8,128)(2,1)S(1)}, u32[]{:S(2)}, u32[]{:S(2)}) collective-permute-start(bf16[528,128]{1,0:T(8,128)(2,1)S(1)} %pack_keys_values.1.message_ref.refs_1_), channel_id=1, source_target_pairs={{0,2},{1,3},{2,0},{3,1},{4,6},{5,7},{6,4},{7,5},{8,10},{9,11},{10,... | collective-permute-start | bytes 405512 | tf_op jit(solution)/shard_map/ppermute | solution.py:209
  10.0 1.3 %collective-permute-done.2.refs_4_ = bf16[528,128]{1,0:T(8,128)(2,1)S(1)} collective-permute-done((bf16[528,128]{1,0:T(8,128)(2,1)S(1)}, bf16[528,128]{1,0:T(8,128)(2,1)S(1)}, u32[]{:S(2)}, u32[]{:S(2)}) %collective-permute-start.2) | collective-permute-done | bytes 135200 | tf_op jit(solution)/shard_map/ppermute | solution.py:209
  11.3 1.7 %collective-permute-start.5 = (bf16[528,128]{1,0:T(8,128)(2,1)S(1)}, bf16[528,128]{1,0:T(8,128)(2,1)S(1)}, u32[]{:S(2)}, u32[]{:S(2)}) collective-permute-start(bf16[528,128]{1,0:T(8,128)(2,1)S(1)} %collective-permute-done.2.refs_4_), channel_id=1, source_target_pairs={{0,2},{1,3},{2,0},{3,1},{4,6},{5,7},{6,4},{7,5},{8,10},{9,11},{10,... | collective-permute-start | bytes 405512 | tf_op jit(solution)/shard_map/ppermute | solution.py:209
  13.0 1.5 %collective-permute-start.3 = (bf16[528,128]{1,0:T(8,128)(2,1)S(1)}, bf16[528,128]{1,0:T(8,128)(2,1)S(1)}, u32[]{:S(2)}, u32[]{:S(2)}) collective-permute-start(bf16[528,128]{1,0:T(8,128)(2,1)S(1)} %collective-permute-done.2.refs_4_), channel_id=1, source_target_pairs={{0,4},{1,5},{2,6},{3,7},{4,0},{5,1},{6,2},{7,3},{8,12},{9,13},{10,... | collective-permute-start | bytes 405512 | tf_op jit(solution)/shard_map/ppermute | solution.py:209
  14.5 0.0 collective-permute-done.1.refs_3_
  14.5 0.5 %collective-permute-start.4 = (bf16[528,128]{1,0:T(8,128)(2,1)S(1)}, bf16[528,128]{1,0:T(8,128)(2,1)S(1)}, u32[]{:S(2)}, u32[]{:S(2)}) collective-permute-start(bf16[528,128]{1,0:T(8,128)(2,1)S(1)} %collective-permute-done.1.refs_3_), channel_id=1, source_target_pairs={{0,2},{1,3},{2,0},{3,1},{4,6},{5,7},{6,4},{7,5},{8,10},{9,11},{10,... | collective-permute-start | bytes 405512 | tf_op jit(solution)/shard_map/ppermute | solution.py:209
  15.0 0.0 collective-permute-done.refs_2_
  15.0 1.5 %collective-permute-start.6 = (bf16[528,128]{1,0:T(8,128)(2,1)S(1)}, bf16[528,128]{1,0:T(8,128)(2,1)S(1)}, u32[]{:S(2)}, u32[]{:S(2)}) collective-permute-start(bf16[528,128]{1,0:T(8,128)(2,1)S(1)} %collective-permute-done.2.refs_4_), channel_id=1, source_target_pairs={{0,6},{1,7},{2,4},{3,5},{4,2},{5,3},{6,0},{7,1},{8,14},{9,15},{10,... | collective-permute-start | bytes 405512 | tf_op jit(solution)/shard_map/ppermute | solution.py:209
  16.5 0.0 collective-permute-done.7.refs_0_
  16.5 0.0 collective-permute-done.5.refs_7_.refs_5_.refs_3_
  16.5 1.2 %absorb_theirs.2 = (f32[128,1024]{1,0:T(8,128)S(1)}, f32[2,1024]{1,0:T(2,128)S(1)}) custom-call(bf16[1040,128]{1,0:T(8,128)(2,1)S(1)} %collective-permute-done.7.refs_0_, bf16[528,128]{1,0:T(8,128)(2,1)S(1)} %pack_keys_values.1.message_ref.refs_1_, bf16[528,128]{1,0:T(8,128)(2,1)S(1)} %collective-permute-done.refs_2_, ...), custom_call_target="tpu_custom_call" | custom-call | flops 268435456 | bytes 1048576 | tf_op jit(solution)/shard_map/absorb_theirs/pallas_call | solution.py:218
  17.7 1.1 %collective-permute-done.3.refs_5_ = bf16[528,128]{1,0:T(8,128)(2,1)S(1)} collective-permute-done((bf16[528,128]{1,0:T(8,128)(2,1)S(1)}, bf16[528,128]{1,0:T(8,128)(2,1)S(1)}, u32[]{:S(2)}, u32[]{:S(2)}) %collective-permute-start.3) | collective-permute-done | bytes 135200 | tf_op jit(solution)/shard_map/ppermute | solution.py:209
  18.9 0.7 %collective-permute-done.4.refs_6_.refs_4_ = bf16[528,128]{1,0:T(8,128)(2,1)S(1)} collective-permute-done((bf16[528,128]{1,0:T(8,128)(2,1)S(1)}, bf16[528,128]{1,0:T(8,128)(2,1)S(1)}, u32[]{:S(2)}, u32[]{:S(2)}) %collective-permute-start.4) | collective-permute-done | bytes 135200 | tf_op jit(solution)/shard_map/ppermute | solution.py:209
  19.5 0.9 %absorb_theirs.3 = (f32[128,1024]{1,0:T(8,128)S(1)}, f32[2,1024]{1,0:T(2,128)S(1)}) custom-call(bf16[1040,128]{1,0:T(8,128)(2,1)S(1)} %collective-permute-done.7.refs_0_, f32[128,1024]{1,0:T(8,128)S(1)} %get-tuple-element.10.refs_1_, f32[2,1024]{1,0:T(2,128)S(1)} %get-tuple-element.11.refs_2_, ...), custom_call_target="tpu_custom_call" | custom-call | flops 201326592 | bytes 1048576 | tf_op jit(solution)/shard_map/absorb_theirs/pallas_call | solution.py:218
  20.5 0.5 %collective-permute-done.6.refs_8_.refs_3_ = bf16[528,128]{1,0:T(8,128)(2,1)S(1)} collective-permute-done((bf16[528,128]{1,0:T(8,128)(2,1)S(1)}, bf16[528,128]{1,0:T(8,128)(2,1)S(1)}, u32[]{:S(2)}, u32[]{:S(2)}) %collective-permute-start.6) | collective-permute-done | bytes 135200 | tf_op jit(solution)/shard_map/ppermute | solution.py:209
  21.0 0.5 %message.1 = bf16[1056,128]{1,0:T(8,128)(2,1)S(1)} custom-call(bf16[1040,128]{1,0:T(8,128)(2,1)S(1)} %collective-permute-done.7.refs_0_, f32[128,1024]{1,0:T(8,128)S(1)} %get-tuple-element.12.refs_1_, f32[2,1024]{1,0:T(2,128)S(1)} %get-tuple-element.13.refs_2_, bf16[528,128]{1,0:T(8,128)(2,1)S(1)} %collective-permute-done.6.refs_8_.refs_3_), custom_call_target="tpu_custom_call" | custom-call | flops 67108864 | bytes 1048576 | tf_op jit(solution)/shard_map/message/pallas_call | solution.py:248
  21.5 1.6 %collective-permute-start.8 = (bf16[1056,128]{1,0:T(8,128)(2,1)S(1)}, bf16[1056,128]{1,0:T(8,128)(2,1)S(1)}, u32[]{:S(2)}, u32[]{:S(2)}) collective-permute-start(bf16[1056,128]{1,0:T(8,128)(2,1)S(1)} %message.1), channel_id=1, source_target_pairs={{0,1},{1,0},{2,3},{3,2},{4,5},{5,4},{6,7},{7,6},{8,9},{9,8},{10,11... | collective-permute-start | bytes 811016 | tf_op jit(solution)/shard_map/ppermute | solution.py:209
  23.0 2.2 %absorb_mine.1 = (f32[128,1024]{1,0:T(8,128)S(1)}, f32[2,1024]{1,0:T(2,128)S(1)}) custom-call(bf16[1040,128]{1,0:T(8,128)(2,1)S(1)} %pack_queries.1.refs_0_, bf16[528,128]{1,0:T(8,128)(2,1)S(1)} %pack_keys_values.1.message_ref.refs_1_, bf16[528,128]{1,0:T(8,128)(2,1)S(1)} %collective-permute-done.refs_2_, ...), custom_call_target="tpu_custom_call" | custom-call | flops 536870912 | bytes 1048576 | tf_op jit(solution)/shard_map/absorb_mine/pallas_call | solution.py:218
  25.2 2.7 %collective-permute-done.8.message_ref = bf16[1056,128]{1,0:T(8,128)(2,1)S(1)} collective-permute-done((bf16[1056,128]{1,0:T(8,128)(2,1)S(1)}, bf16[1056,128]{1,0:T(8,128)(2,1)S(1)}, u32[]{:S(2)}, u32[]{:S(2)}) %collective-permute-start.8) | collective-permute-done | bytes 270368 | tf_op jit(solution)/shard_map/ppermute | solution.py:209
  28.0 0.9 %finish.1 = (bf16[128,1024]{1,0:T(8,128)(2,1)}, f32[8,128]{1,0:T(8,128)}) custom-call(f32[128,1024]{1,0:T(8,128)S(1)} %get-tuple-element.8.acc_ref, f32[2,1024]{1,0:T(2,128)S(1)} %get-tuple-element.9.stat_ref, bf16[1056,128]{1,0:T(8,128)(2,1)S(1)} %collective-permute-done.8.message_ref), custom_call_target="tpu_custom_call" | custom-call | bytes 1048576 | tf_op jit(solution)/shard_map/finish/pallas_call | solution.py:260
Async XLA Ops:
  0.6 6.2 %copy-start = (bf16[128,1024]{1,0:T(8,128)(2,1)S(1)}, bf16[128,1024]{1,0:T(8,128)(2,1)}, u32[]{:S(2)}) copy-start(bf16[128,1024]{1,0:T(8,128)(2,1)} %queries_ref.1) | copy-start | bytes 786436
  1.7 9.6 %collective-permute-start.2 = (bf16[528,128]{1,0:T(8,128)(2,1)S(1)}, bf16[528,128]{1,0:T(8,128)(2,1)S(1)}, u32[]{:S(2)}, u32[]{:S(2)}) collective-permute-start(bf16[528,128]{1,0:T(8,128)(2,1)S(1)} %pack_keys_values.1.message_ref.refs_1_), channel_id=1, source_target_pairs={{0,12},{1,13},{2,14},{3,15},{4,8},{5,9},{6,10},{7,11},{8,4},{9,5},... | collective-permute-start | bytes 405512 | tf_op jit(solution)/shard_map/ppermute | solution.py:209
  6.9 9.6 %collective-permute-start.7 = (bf16[1040,128]{1,0:T(8,128)(2,1)S(1)}, bf16[1040,128]{1,0:T(8,128)(2,1)S(1)}, u32[]{:S(2)}, u32[]{:S(2)}) collective-permute-start(bf16[1040,128]{1,0:T(8,128)(2,1)S(1)} %pack_queries.1.refs_0_), channel_id=1, source_target_pairs={{0,1},{1,0},{2,3},{3,2},{4,5},{5,4},{6,7},{7,6},{8,9},{9,8},{10,11... | collective-permute-start | bytes 798728 | tf_op jit(solution)/shard_map/ppermute | solution.py:209
  8.5 6.0 %collective-permute-start.1 = (bf16[528,128]{1,0:T(8,128)(2,1)S(1)}, bf16[528,128]{1,0:T(8,128)(2,1)S(1)}, u32[]{:S(2)}, u32[]{:S(2)}) collective-permute-start(bf16[528,128]{1,0:T(8,128)(2,1)S(1)} %pack_keys_values.1.message_ref.refs_1_), channel_id=1, source_target_pairs={{0,4},{1,5},{2,6},{3,7},{4,0},{5,1},{6,2},{7,3},{8,12},{9,13},{10,... | collective-permute-start | bytes 405512 | tf_op jit(solution)/shard_map/ppermute | solution.py:209
  8.5 6.5 %collective-permute-start = (bf16[528,128]{1,0:T(8,128)(2,1)S(1)}, bf16[528,128]{1,0:T(8,128)(2,1)S(1)}, u32[]{:S(2)}, u32[]{:S(2)}) collective-permute-start(bf16[528,128]{1,0:T(8,128)(2,1)S(1)} %pack_keys_values.1.message_ref.refs_1_), channel_id=1, source_target_pairs={{0,2},{1,3},{2,0},{3,1},{4,6},{5,7},{6,4},{7,5},{8,10},{9,11},{10,... | collective-permute-start | bytes 405512 | tf_op jit(solution)/shard_map/ppermute | solution.py:209
  11.3 5.3 %collective-permute-start.5 = (bf16[528,128]{1,0:T(8,128)(2,1)S(1)}, bf16[528,128]{1,0:T(8,128)(2,1)S(1)}, u32[]{:S(2)}, u32[]{:S(2)}) collective-permute-start(bf16[528,128]{1,0:T(8,128)(2,1)S(1)} %collective-permute-done.2.refs_4_), channel_id=1, source_target_pairs={{0,2},{1,3},{2,0},{3,1},{4,6},{5,7},{6,4},{7,5},{8,10},{9,11},{10,... | collective-permute-start | bytes 405512 | tf_op jit(solution)/shard_map/ppermute | solution.py:209
  13.0 5.9 %collective-permute-start.3 = (bf16[528,128]{1,0:T(8,128)(2,1)S(1)}, bf16[528,128]{1,0:T(8,128)(2,1)S(1)}, u32[]{:S(2)}, u32[]{:S(2)}) collective-permute-start(bf16[528,128]{1,0:T(8,128)(2,1)S(1)} %collective-permute-done.2.refs_4_), channel_id=1, source_target_pairs={{0,4},{1,5},{2,6},{3,7},{4,0},{5,1},{6,2},{7,3},{8,12},{9,13},{10,... | collective-permute-start | bytes 405512 | tf_op jit(solution)/shard_map/ppermute | solution.py:209
  14.5 5.0 %collective-permute-start.4 = (bf16[528,128]{1,0:T(8,128)(2,1)S(1)}, bf16[528,128]{1,0:T(8,128)(2,1)S(1)}, u32[]{:S(2)}, u32[]{:S(2)}) collective-permute-start(bf16[528,128]{1,0:T(8,128)(2,1)S(1)} %collective-permute-done.1.refs_3_), channel_id=1, source_target_pairs={{0,2},{1,3},{2,0},{3,1},{4,6},{5,7},{6,4},{7,5},{8,10},{9,11},{10,... | collective-permute-start | bytes 405512 | tf_op jit(solution)/shard_map/ppermute | solution.py:209
  15.0 6.0 %collective-permute-start.6 = (bf16[528,128]{1,0:T(8,128)(2,1)S(1)}, bf16[528,128]{1,0:T(8,128)(2,1)S(1)}, u32[]{:S(2)}, u32[]{:S(2)}) collective-permute-start(bf16[528,128]{1,0:T(8,128)(2,1)S(1)} %collective-permute-done.2.refs_4_), channel_id=1, source_target_pairs={{0,6},{1,7},{2,4},{3,5},{4,2},{5,3},{6,0},{7,1},{8,14},{9,15},{10,... | collective-permute-start | bytes 405512 | tf_op jit(solution)/shard_map/ppermute | solution.py:209
  21.5 6.5 %collective-permute-start.8 = (bf16[1056,128]{1,0:T(8,128)(2,1)S(1)}, bf16[1056,128]{1,0:T(8,128)(2,1)S(1)}, u32[]{:S(2)}, u32[]{:S(2)}) collective-permute-start(bf16[1056,128]{1,0:T(8,128)(2,1)S(1)} %message.1), channel_id=1, source_target_pairs={{0,1},{1,0},{2,3},{3,2},{4,5},{5,4},{6,7},{7,6},{8,9},{9,8},{10,11... | collective-permute-start | bytes 811016 | tf_op jit(solution)/shard_map/ppermute | solution.py:209

commit v3 on v2

--- a/solution.py
+++ b/solution.py
@@ -42,43 +42,32 @@
     return jnp.where(row == 0, high, jnp.where(row == 1, low, 0)).astype(jnp.float32).astype(jnp.bfloat16)
 
 
-def pack_kernel(turned, *refs):
-    sources, pos_hbm, out_ref, pos_ref, held_ref, sems = refs[: len(turned)], *refs[len(turned) :]
+def pack_kernel(heads, *refs):
+    sources, pos_hbm, out_ref, pos_ref, sems = refs[: len(heads)], *refs[len(heads) :]
     rows = pos_hbm.shape[0]
     copies = [pltpu.make_async_copy(pos_hbm, pos_ref, sems.at[0])]
-    moves = []
-    for source, (count, turn) in zip(sources, turned):
+    for source, count in zip(sources, heads):
         for head in range(count):
             index = len(copies) - 1
-            place = pl.ds(index * rows, rows)
-            target = held_ref if turn else out_ref
-            copies.append(
-                pltpu.make_async_copy(source.at[:, pl.ds(head * HD, HD)], target.at[place, :], sems.at[index + 1])
-            )
-            moves.append(place if turn else None)
+            place = out_ref.at[pl.ds(index * rows, rows), :]
+            copies.append(pltpu.make_async_copy(source.at[:, pl.ds(head * HD, HD)], place, sems.at[index + 1]))
     for copy in copies:
         copy.start()
     copies[0].wait()
     out_ref[out_ref.shape[0] - TAIL :, :] = position_rows(pos_ref)
-    for copy, place in zip(copies[1:], moves):
+    for copy in copies[1:]:
         copy.wait()
-        if place is not None:
-            out_ref[place, :] = held_ref[place, :].T
-
-
-def pack(name, sources, turned, positions):
+
+
+def pack(name, sources, heads, positions):
     rows = positions.shape[0]
-    count = sum(heads for heads, unused in turned)
+    count = sum(heads)
     return pl.pallas_call(
-        functools.partial(pack_kernel, turned),
+        functools.partial(pack_kernel, heads),
         out_shape=jax.ShapeDtypeStruct((count * rows + TAIL, HD), jnp.bfloat16),
         in_specs=[pl.BlockSpec(memory_space=pltpu.HBM)] * (len(sources) + 1),
         out_specs=VMEM,
-        scratch_shapes=[
-            pltpu.VMEM((rows,), jnp.int32),
-            pltpu.VMEM((count * rows, HD), jnp.bfloat16),
-            pltpu.SemaphoreType.DMA((count + 1,)),
-        ],
+        scratch_shapes=[pltpu.VMEM((rows,), jnp.int32), pltpu.SemaphoreType.DMA((count + 1,))],
         compiler_params=pltpu.CompilerParams(vmem_limit_bytes=32 * 1024 * 1024),
         cost_estimate=pl.CostEstimate(flops=0, bytes_accessed=count * rows * HD * 4, transcendentals=0),
         name=name,
@@ -133,7 +122,9 @@
             weights = jnp.exp2(part * SCALE - peak)
             sums = weights if sums is None else sums + weights
             block_values = ref[base + (KVH + group) * rows : base + (KVH + group + 1) * rows, :]
-            update = jnp.dot(block_values, weights.astype(jnp.bfloat16), preferred_element_type=jnp.float32)
+            update = lax.dot_general(
+                block_values, weights.astype(jnp.bfloat16), (((0,), (0,)), ((), ())), preferred_element_type=jnp.float32
+            )
             accumulated = update if accumulated is None else accumulated + update
         total = jnp.sum(sums, axis=0, keepdims=True)
         if state is not None:
@@ -217,7 +208,7 @@
         inputs = [query, *state_of, *arrays, *after]
         return call(kernel, list(state), name, flops * sum(map(len, bases)), len(inputs))(*inputs)
 
-    kv = pack("pack_keys_values", (keys, values), ((KVH, False), (KVH, True)), positions)
+    kv = pack("pack_keys_values", (keys, values), (KVH, KVH), positions)
     q = call(pack_queries_kernel, jax.ShapeDtypeStruct((QH * rows + TAIL, HD), bf16), "pack_queries", 0, 2)(queries, kv)
     if ctx == 16:
         near, far, side, other_side = 4, 12, (1, 2), (2, 1)

time: 29 us -> 28.9 us (level)
  no operation moved by 1% of the time
where the time goes in v3:
time: 28.9 us; the launch traced here: 28.8 us
  starting transfers between devices  15 us (52%)
  Pallas kernels  6.83 us (24%)
  waiting for transfers between devices  6.24 us (22%)
  between operations  0.69 us (2%)
    ppermute x9, starting transfers between devices, exchange(): return lax.ppermute(array, AXES, pairs)  15 us
    ppermute x9, waiting for transfers between devices, exchange(): return lax.ppermute(array, AXES, pairs)  6.24 us
    pallas_call x3, Pallas kernels, absorb_call(): call(kernel, list(state), name, flops * sum(map(len, bases)), len(inputs))  4.41 us
    pallas_call x1, Pallas kernels, shards(): call(functools.partial(finish_kernel, rows), outs, 'finish', 0, 3)  0.91 us
    pallas_call x1, Pallas kernels, pack(): pl.pallas_call(functools.partial(pack_kernel, heads), out_shape=jax.Shape...  0.91 us
  transfers between devices with their start and end apart: 9, of which 5 were waited for; matrix products, arithmetic and copies ran while one was open for 0% of the time, Pallas kernels for 16%

profile of v3, /device:TPU:0, one launch (start us, length us, event | category | flops | bytes accessed | tf_op | source)
XLA Modules:
  0.0 28.8 jit_solution(3868642584532779819)
XLA Ops:
  0.6 0.0 copy-start
  0.6 0.9 %pack_keys_values.1.message_ref.refs_1_ = bf16[528,128]{1,0:T(8,128)(2,1)S(1)} custom-call(bf16[128,256]{1,0:T(8,128)(2,1)} %refs_0_.1, bf16[128,256]{1,0:T(8,128)(2,1)} %refs_1_.1, s32[128]{0:T(128)} %refs_2_.1), custom_call_target="tpu_custom_call" | custom-call | bytes 262144 | tf_op jit(solution)/shard_map/pack_keys_values/pallas_call | solution.py:65
  1.6 5.1 %collective-permute-start.2 = (bf16[528,128]{1,0:T(8,128)(2,1)S(1)}, bf16[528,128]{1,0:T(8,128)(2,1)S(1)}, u32[]{:S(2)}, u32[]{:S(2)}) collective-permute-start(bf16[528,128]{1,0:T(8,128)(2,1)S(1)} %pack_keys_values.1.message_ref.refs_1_), channel_id=1, source_target_pairs={{0,12},{1,13},{2,14},{3,15},{4,8},{5,9},{6,10},{7,11},{8,4},{9,5},... | collective-permute-start | bytes 405512 | tf_op jit(solution)/shard_map/ppermute | solution.py:200
  6.7 0.0 copy-done
  6.7 0.1 pack_queries.1.refs_0_
  6.8 1.6 %collective-permute-start.7 = (bf16[1040,128]{1,0:T(8,128)(2,1)S(1)}, bf16[1040,128]{1,0:T(8,128)(2,1)S(1)}, u32[]{:S(2)}, u32[]{:S(2)}) collective-permute-start(bf16[1040,128]{1,0:T(8,128)(2,1)S(1)} %pack_queries.1.refs_0_), channel_id=1, source_target_pairs={{0,1},{1,0},{2,3},{3,2},{4,5},{5,4},{6,7},{7,6},{8,9},{9,8},{10,11... | collective-permute-start | bytes 798728 | tf_op jit(solution)/shard_map/ppermute | solution.py:200
  8.4 0.0 collective-permute-start.1
  8.4 1.5 %collective-permute-start = (bf16[528,128]{1,0:T(8,128)(2,1)S(1)}, bf16[528,128]{1,0:T(8,128)(2,1)S(1)}, u32[]{:S(2)}, u32[]{:S(2)}) collective-permute-start(bf16[528,128]{1,0:T(8,128)(2,1)S(1)} %pack_keys_values.1.message_ref.refs_1_), channel_id=1, source_target_pairs={{0,2},{1,3},{2,0},{3,1},{4,6},{5,7},{6,4},{7,5},{8,10},{9,11},{10,... | collective-permute-start | bytes 405512 | tf_op jit(solution)/shard_map/ppermute | solution.py:200
  9.9 1.3 %collective-permute-done.2.refs_4_ = bf16[528,128]{1,0:T(8,128)(2,1)S(1)} collective-permute-done((bf16[528,128]{1,0:T(8,128)(2,1)S(1)}, bf16[528,128]{1,0:T(8,128)(2,1)S(1)}, u32[]{:S(2)}, u32[]{:S(2)}) %collective-permute-start.2) | collective-permute-done | bytes 135200 | tf_op jit(solution)/shard_map/ppermute | solution.py:200
  11.1 1.7 %collective-permute-start.5 = (bf16[528,128]{1,0:T(8,128)(2,1)S(1)}, bf16[528,128]{1,0:T(8,128)(2,1)S(1)}, u32[]{:S(2)}, u32[]{:S(2)}) collective-permute-start(bf16[528,128]{1,0:T(8,128)(2,1)S(1)} %collective-permute-done.2.refs_4_), channel_id=1, source_target_pairs={{0,2},{1,3},{2,0},{3,1},{4,6},{5,7},{6,4},{7,5},{8,10},{9,11},{10,... | collective-permute-start | bytes 405512 | tf_op jit(solution)/shard_map/ppermute | solution.py:200
  12.9 1.5 %collective-permute-start.3 = (bf16[528,128]{1,0:T(8,128)(2,1)S(1)}, bf16[528,128]{1,0:T(8,128)(2,1)S(1)}, u32[]{:S(2)}, u32[]{:S(2)}) collective-permute-start(bf16[528,128]{1,0:T(8,128)(2,1)S(1)} %collective-permute-done.2.refs_4_), channel_id=1, source_target_pairs={{0,4},{1,5},{2,6},{3,7},{4,0},{5,1},{6,2},{7,3},{8,12},{9,13},{10,... | collective-permute-start | bytes 405512 | tf_op jit(solution)/shard_map/ppermute | solution.py:200
  14.4 0.0 collective-permute-done.1.refs_3_
  14.4 0.5 %collective-permute-start.4 = (bf16[528,128]{1,0:T(8,128)(2,1)S(1)}, bf16[528,128]{1,0:T(8,128)(2,1)S(1)}, u32[]{:S(2)}, u32[]{:S(2)}) collective-permute-start(bf16[528,128]{1,0:T(8,128)(2,1)S(1)} %collective-permute-done.1.refs_3_), channel_id=1, source_target_pairs={{0,2},{1,3},{2,0},{3,1},{4,6},{5,7},{6,4},{7,5},{8,10},{9,11},{10,... | collective-permute-start | bytes 405512 | tf_op jit(solution)/shard_map/ppermute | solution.py:200
  14.9 0.0 collective-permute-done.refs_2_
  14.9 1.5 %collective-permute-start.6 = (bf16[528,128]{1,0:T(8,128)(2,1)S(1)}, bf16[528,128]{1,0:T(8,128)(2,1)S(1)}, u32[]{:S(2)}, u32[]{:S(2)}) collective-permute-start(bf16[528,128]{1,0:T(8,128)(2,1)S(1)} %collective-permute-done.2.refs_4_), channel_id=1, source_target_pairs={{0,6},{1,7},{2,4},{3,5},{4,2},{5,3},{6,0},{7,1},{8,14},{9,15},{10,... | collective-permute-start | bytes 405512 | tf_op jit(solution)/shard_map/ppermute | solution.py:200
  16.4 0.0 collective-permute-done.7.refs_0_
  16.4 0.0 collective-permute-done.5.refs_7_.refs_5_.refs_3_
  16.4 1.2 %absorb_theirs.2 = (f32[128,1024]{1,0:T(8,128)S(1)}, f32[2,1024]{1,0:T(2,128)S(1)}) custom-call(bf16[1040,128]{1,0:T(8,128)(2,1)S(1)} %collective-permute-done.7.refs_0_, bf16[528,128]{1,0:T(8,128)(2,1)S(1)} %pack_keys_values.1.message_ref.refs_1_, bf16[528,128]{1,0:T(8,128)(2,1)S(1)} %collective-permute-done.refs_2_, ...), custom_call_target="tpu_custom_call" | custom-call | flops 268435456 | bytes 1048576 | tf_op jit(solution)/shard_map/absorb_theirs/pallas_call | solution.py:209
  17.6 1.1 %collective-permute-done.3.refs_5_ = bf16[528,128]{1,0:T(8,128)(2,1)S(1)} collective-permute-done((bf16[528,128]{1,0:T(8,128)(2,1)S(1)}, bf16[528,128]{1,0:T(8,128)(2,1)S(1)}, u32[]{:S(2)}, u32[]{:S(2)}) %collective-permute-start.3) | collective-permute-done | bytes 135200 | tf_op jit(solution)/shard_map/ppermute | solution.py:200
  18.8 0.7 %collective-permute-done.4.refs_6_.refs_4_ = bf16[528,128]{1,0:T(8,128)(2,1)S(1)} collective-permute-done((bf16[528,128]{1,0:T(8,128)(2,1)S(1)}, bf16[528,128]{1,0:T(8,128)(2,1)S(1)}, u32[]{:S(2)}, u32[]{:S(2)}) %collective-permute-start.4) | collective-permute-done | bytes 135200 | tf_op jit(solution)/shard_map/ppermute | solution.py:200
  19.4 1.0 %absorb_theirs.3 = (f32[128,1024]{1,0:T(8,128)S(1)}, f32[2,1024]{1,0:T(2,128)S(1)}) custom-call(bf16[1040,128]{1,0:T(8,128)(2,1)S(1)} %collective-permute-done.7.refs_0_, f32[128,1024]{1,0:T(8,128)S(1)} %get-tuple-element.10.refs_1_, f32[2,1024]{1,0:T(2,128)S(1)} %get-tuple-element.11.refs_2_, ...), custom_call_target="tpu_custom_call" | custom-call | flops 201326592 | bytes 1048576 | tf_op jit(solution)/shard_map/absorb_theirs/pallas_call | solution.py:209
  20.4 0.5 %collective-permute-done.6.refs_8_.refs_3_ = bf16[528,128]{1,0:T(8,128)(2,1)S(1)} collective-permute-done((bf16[528,128]{1,0:T(8,128)(2,1)S(1)}, bf16[528,128]{1,0:T(8,128)(2,1)S(1)}, u32[]{:S(2)}, u32[]{:S(2)}) %collective-permute-start.6) | collective-permute-done | bytes 135200 | tf_op jit(solution)/shard_map/ppermute | solution.py:200
  20.9 0.5 %message.1 = bf16[1056,128]{1,0:T(8,128)(2,1)S(1)} custom-call(bf16[1040,128]{1,0:T(8,128)(2,1)S(1)} %collective-permute-done.7.refs_0_, f32[128,1024]{1,0:T(8,128)S(1)} %get-tuple-element.12.refs_1_, f32[2,1024]{1,0:T(2,128)S(1)} %get-tuple-element.13.refs_2_, bf16[528,128]{1,0:T(8,128)(2,1)S(1)} %collective-permute-done.6.refs_8_.refs_3_), custom_call_target="tpu_custom_call" | custom-call | flops 67108864 | bytes 1048576 | tf_op jit(solution)/shard_map/message/pallas_call | solution.py:239
  21.3 1.6 %collective-permute-start.8 = (bf16[1056,128]{1,0:T(8,128)(2,1)S(1)}, bf16[1056,128]{1,0:T(8,128)(2,1)S(1)}, u32[]{:S(2)}, u32[]{:S(2)}) collective-permute-start(bf16[1056,128]{1,0:T(8,128)(2,1)S(1)} %message.1), channel_id=1, source_target_pairs={{0,1},{1,0},{2,3},{3,2},{4,5},{5,4},{6,7},{7,6},{8,9},{9,8},{10,11... | collective-permute-start | bytes 811016 | tf_op jit(solution)/shard_map/ppermute | solution.py:200
  22.9 2.2 %absorb_mine.1 = (f32[128,1024]{1,0:T(8,128)S(1)}, f32[2,1024]{1,0:T(2,128)S(1)}) custom-call(bf16[1040,128]{1,0:T(8,128)(2,1)S(1)} %pack_queries.1.refs_0_, bf16[528,128]{1,0:T(8,128)(2,1)S(1)} %pack_keys_values.1.message_ref.refs_1_, bf16[528,128]{1,0:T(8,128)(2,1)S(1)} %collective-permute-done.refs_2_, ...), custom_call_target="tpu_custom_call" | custom-call | flops 536870912 | bytes 1048576 | tf_op jit(solution)/shard_map/absorb_mine/pallas_call | solution.py:209
  25.1 2.7 %collective-permute-done.8.message_ref = bf16[1056,128]{1,0:T(8,128)(2,1)S(1)} collective-permute-done((bf16[1056,128]{1,0:T(8,128)(2,1)S(1)}, bf16[1056,128]{1,0:T(8,128)(2,1)S(1)}, u32[]{:S(2)}, u32[]{:S(2)}) %collective-permute-start.8) | collective-permute-done | bytes 270368 | tf_op jit(solution)/shard_map/ppermute | solution.py:200
  27.9 0.9 %finish.1 = (bf16[128,1024]{1,0:T(8,128)(2,1)}, f32[8,128]{1,0:T(8,128)}) custom-call(f32[128,1024]{1,0:T(8,128)S(1)} %get-tuple-element.8.acc_ref, f32[2,1024]{1,0:T(2,128)S(1)} %get-tuple-element.9.stat_ref, bf16[1056,128]{1,0:T(8,128)(2,1)S(1)} %collective-permute-done.8.message_ref), custom_call_target="tpu_custom_call" | custom-call | bytes 1048576 | tf_op jit(solution)/shard_map/finish/pallas_call | solution.py:251
Async XLA Ops:
  0.6 6.0 %copy-start = (bf16[128,1024]{1,0:T(8,128)(2,1)S(1)}, bf16[128,1024]{1,0:T(8,128)(2,1)}, u32[]{:S(2)}) copy-start(bf16[128,1024]{1,0:T(8,128)(2,1)} %queries_ref.1) | copy-start | bytes 786436
  1.6 9.6 %collective-permute-start.2 = (bf16[528,128]{1,0:T(8,128)(2,1)S(1)}, bf16[528,128]{1,0:T(8,128)(2,1)S(1)}, u32[]{:S(2)}, u32[]{:S(2)}) collective-permute-start(bf16[528,128]{1,0:T(8,128)(2,1)S(1)} %pack_keys_values.1.message_ref.refs_1_), channel_id=1, source_target_pairs={{0,12},{1,13},{2,14},{3,15},{4,8},{5,9},{6,10},{7,11},{8,4},{9,5},... | collective-permute-start | bytes 405512 | tf_op jit(solution)/shard_map/ppermute | solution.py:200
  6.8 9.6 %collective-permute-start.7 = (bf16[1040,128]{1,0:T(8,128)(2,1)S(1)}, bf16[1040,128]{1,0:T(8,128)(2,1)S(1)}, u32[]{:S(2)}, u32[]{:S(2)}) collective-permute-start(bf16[1040,128]{1,0:T(8,128)(2,1)S(1)} %pack_queries.1.refs_0_), channel_id=1, source_target_pairs={{0,1},{1,0},{2,3},{3,2},{4,5},{5,4},{6,7},{7,6},{8,9},{9,8},{10,11... | collective-permute-start | bytes 798728 | tf_op jit(solution)/shard_map/ppermute | solution.py:200
  8.4 6.0 %collective-permute-start.1 = (bf16[528,128]{1,0:T(8,128)(2,1)S(1)}, bf16[528,128]{1,0:T(8,128)(2,1)S(1)}, u32[]{:S(2)}, u32[]{:S(2)}) collective-permute-start(bf16[528,128]{1,0:T(8,128)(2,1)S(1)} %pack_keys_values.1.message_ref.refs_1_), channel_id=1, source_target_pairs={{0,4},{1,5},{2,6},{3,7},{4,0},{5,1},{6,2},{7,3},{8,12},{9,13},{10,... | collective-permute-start | bytes 405512 | tf_op jit(solution)/shard_map/ppermute | solution.py:200
  8.4 6.5 %collective-permute-start = (bf16[528,128]{1,0:T(8,128)(2,1)S(1)}, bf16[528,128]{1,0:T(8,128)(2,1)S(1)}, u32[]{:S(2)}, u32[]{:S(2)}) collective-permute-start(bf16[528,128]{1,0:T(8,128)(2,1)S(1)} %pack_keys_values.1.message_ref.refs_1_), channel_id=1, source_target_pairs={{0,2},{1,3},{2,0},{3,1},{4,6},{5,7},{6,4},{7,5},{8,10},{9,11},{10,... | collective-permute-start | bytes 405512 | tf_op jit(solution)/shard_map/ppermute | solution.py:200
  11.1 5.3 %collective-permute-start.5 = (bf16[528,128]{1,0:T(8,128)(2,1)S(1)}, bf16[528,128]{1,0:T(8,128)(2,1)S(1)}, u32[]{:S(2)}, u32[]{:S(2)}) collective-permute-start(bf16[528,128]{1,0:T(8,128)(2,1)S(1)} %collective-permute-done.2.refs_4_), channel_id=1, source_target_pairs={{0,2},{1,3},{2,0},{3,1},{4,6},{5,7},{6,4},{7,5},{8,10},{9,11},{10,... | collective-permute-start | bytes 405512 | tf_op jit(solution)/shard_map/ppermute | solution.py:200
  12.9 5.9 %collective-permute-start.3 = (bf16[528,128]{1,0:T(8,128)(2,1)S(1)}, bf16[528,128]{1,0:T(8,128)(2,1)S(1)}, u32[]{:S(2)}, u32[]{:S(2)}) collective-permute-start(bf16[528,128]{1,0:T(8,128)(2,1)S(1)} %collective-permute-done.2.refs_4_), channel_id=1, source_target_pairs={{0,4},{1,5},{2,6},{3,7},{4,0},{5,1},{6,2},{7,3},{8,12},{9,13},{10,... | collective-permute-start | bytes 405512 | tf_op jit(solution)/shard_map/ppermute | solution.py:200
  14.4 5.0 %collective-permute-start.4 = (bf16[528,128]{1,0:T(8,128)(2,1)S(1)}, bf16[528,128]{1,0:T(8,128)(2,1)S(1)}, u32[]{:S(2)}, u32[]{:S(2)}) collective-permute-start(bf16[528,128]{1,0:T(8,128)(2,1)S(1)} %collective-permute-done.1.refs_3_), channel_id=1, source_target_pairs={{0,2},{1,3},{2,0},{3,1},{4,6},{5,7},{6,4},{7,5},{8,10},{9,11},{10,... | collective-permute-start | bytes 405512 | tf_op jit(solution)/shard_map/ppermute | solution.py:200
  14.9 6.0 %collective-permute-start.6 = (bf16[528,128]{1,0:T(8,128)(2,1)S(1)}, bf16[528,128]{1,0:T(8,128)(2,1)S(1)}, u32[]{:S(2)}, u32[]{:S(2)}) collective-permute-start(bf16[528,128]{1,0:T(8,128)(2,1)S(1)} %collective-permute-done.2.refs_4_), channel_id=1, source_target_pairs={{0,6},{1,7},{2,4},{3,5},{4,2},{5,3},{6,0},{7,1},{8,14},{9,15},{10,... | collective-permute-start | bytes 405512 | tf_op jit(solution)/shard_map/ppermute | solution.py:200
  21.3 6.5 %collective-permute-start.8 = (bf16[1056,128]{1,0:T(8,128)(2,1)S(1)}, bf16[1056,128]{1,0:T(8,128)(2,1)S(1)}, u32[]{:S(2)}, u32[]{:S(2)}) collective-permute-start(bf16[1056,128]{1,0:T(8,128)(2,1)S(1)} %message.1), channel_id=1, source_target_pairs={{0,1},{1,0},{2,3},{3,2},{4,5},{5,4},{6,7},{7,6},{8,9},{9,8},{10,11... | collective-permute-start | bytes 811016 | tf_op jit(solution)/shard_map/ppermute | solution.py:200

commit v4 on v3

--- a/solution.py
+++ b/solution.py
@@ -18,7 +18,7 @@
 LOWEST = -1e25
 SCALE = HD ** (-0.5) * math.log2(math.e)
 LN2 = math.log(2.0)
-WIDTH = 2
+WIDTH = 1
 AXES = ("dp", "ctx")
 VMEM = pl.BlockSpec(memory_space=pltpu.VMEM)
 
@@ -184,7 +184,7 @@
         log_ref[head : head + 1, :] = joint * LN2
         block = acc_ref[:, lanes] * jnp.exp2(peak - joint)
         other = message_ref[lanes, :].astype(jnp.float32) * jnp.exp2(their - joint)
-        attended_ref[:, head * HD : (head + 1) * HD] = (block + other).T.astype(jnp.bfloat16)
+        attended_ref[:, head * HD : (head + 1) * HD] = (block + other).astype(jnp.bfloat16).T
 
 
 def shards(dp, ctx, queries, keys, values, positions):

time: 28.9 us -> 28.9 us (level)
  Pallas kernels: 6.83 us -> 6.49 us
  waiting for transfers between devices: 6.24 us -> 6.53 us
    pallas_call x3, Pallas kernels: 4.41 us -> 4.11 us  [absorb_call(): call(kernel, list(state), name, flops * sum(map(len, bases)), len(inputs))]
    ppermute x9, waiting for transfers between devices: 6.24 us -> 6.53 us  [exchange(): return lax.ppermute(array, AXES, pairs)]
  transfers between devices with their start and end apart: 9 -> 9, of which waited for: 5 -> 5; matrix products, arithmetic and copies ran while one was open for 0% -> 0% of each run, Pallas kernels for 16% -> 15%
where the time goes in v4:
time: 28.9 us; the launch traced here: 28.7 us
  starting transfers between devices  15 us (52%)
  waiting for transfers between devices  6.53 us (23%)
  Pallas kernels  6.49 us (22%)
  between operations  0.69 us (2%)
    ppermute x9, starting transfers between devices, exchange(): return lax.ppermute(array, AXES, pairs)  15 us
    ppermute x9, waiting for transfers between devices, exchange(): return lax.ppermute(array, AXES, pairs)  6.53 us
    pallas_call x3, Pallas kernels, absorb_call(): call(kernel, list(state), name, flops * sum(map(len, bases)), len(inputs))  4.11 us
    pallas_call x1, Pallas kernels, pack(): pl.pallas_call(functools.partial(pack_kernel, heads), out_shape=jax.Shape...  0.91 us
    pallas_call x1, Pallas kernels, shards(): call(functools.partial(finish_kernel, rows), outs, 'finish', 0, 3)  0.89 us
  transfers between devices with their start and end apart: 9, of which 5 were waited for; matrix products, arithmetic and copies ran while one was open for 0% of the time, Pallas kernels for 15%

profile of v4, /device:TPU:0, one launch (start us, length us, event | category | flops | bytes accessed | tf_op | source)
XLA Modules:
  0.0 28.7 jit_solution(16465613794763191310)
XLA Ops:
  0.6 0.0 copy-start
  0.6 0.9 %pack_keys_values.1.message_ref.refs_1_ = bf16[528,128]{1,0:T(8,128)(2,1)S(1)} custom-call(bf16[128,256]{1,0:T(8,128)(2,1)} %refs_0_.1, bf16[128,256]{1,0:T(8,128)(2,1)} %refs_1_.1, s32[128]{0:T(128)} %refs_2_.1), custom_call_target="tpu_custom_call" | custom-call | bytes 262144 | tf_op jit(solution)/shard_map/pack_keys_values/pallas_call | solution.py:65
  1.6 5.1 %collective-permute-start.2 = (bf16[528,128]{1,0:T(8,128)(2,1)S(1)}, bf16[528,128]{1,0:T(8,128)(2,1)S(1)}, u32[]{:S(2)}, u32[]{:S(2)}) collective-permute-start(bf16[528,128]{1,0:T(8,128)(2,1)S(1)} %pack_keys_values.1.message_ref.refs_1_), channel_id=1, source_target_pairs={{0,12},{1,13},{2,14},{3,15},{4,8},{5,9},{6,10},{7,11},{8,4},{9,5},... | collective-permute-start | bytes 405512 | tf_op jit(solution)/shard_map/ppermute | solution.py:200
  6.7 0.0 copy-done
  6.7 0.1 pack_queries.1.refs_0_
  6.8 1.6 %collective-permute-start.7 = (bf16[1040,128]{1,0:T(8,128)(2,1)S(1)}, bf16[1040,128]{1,0:T(8,128)(2,1)S(1)}, u32[]{:S(2)}, u32[]{:S(2)}) collective-permute-start(bf16[1040,128]{1,0:T(8,128)(2,1)S(1)} %pack_queries.1.refs_0_), channel_id=1, source_target_pairs={{0,1},{1,0},{2,3},{3,2},{4,5},{5,4},{6,7},{7,6},{8,9},{9,8},{10,11... | collective-permute-start | bytes 798728 | tf_op jit(solution)/shard_map/ppermute | solution.py:200
  8.4 0.0 collective-permute-start.1
  8.4 1.5 %collective-permute-start = (bf16[528,128]{1,0:T(8,128)(2,1)S(1)}, bf16[528,128]{1,0:T(8,128)(2,1)S(1)}, u32[]{:S(2)}, u32[]{:S(2)}) collective-permute-start(bf16[528,128]{1,0:T(8,128)(2,1)S(1)} %pack_keys_values.1.message_ref.refs_1_), channel_id=1, source_target_pairs={{0,2},{1,3},{2,0},{3,1},{4,6},{5,7},{6,4},{7,5},{8,10},{9,11},{10,... | collective-permute-start | bytes 405512 | tf_op jit(solution)/shard_map/ppermute | solution.py:200
  9.9 1.3 %collective-permute-done.2.refs_4_ = bf16[528,128]{1,0:T(8,128)(2,1)S(1)} collective-permute-done((bf16[528,128]{1,0:T(8,128)(2,1)S(1)}, bf16[528,128]{1,0:T(8,128)(2,1)S(1)}, u32[]{:S(2)}, u32[]{:S(2)}) %collective-permute-start.2) | collective-permute-done | bytes 135200 | tf_op jit(solution)/shard_map/ppermute | solution.py:200
  11.1 1.7 %collective-permute-start.5 = (bf16[528,128]{1,0:T(8,128)(2,1)S(1)}, bf16[528,128]{1,0:T(8,128)(2,1)S(1)}, u32[]{:S(2)}, u32[]{:S(2)}) collective-permute-start(bf16[528,128]{1,0:T(8,128)(2,1)S(1)} %collective-permute-done.2.refs_4_), channel_id=1, source_target_pairs={{0,2},{1,3},{2,0},{3,1},{4,6},{5,7},{6,4},{7,5},{8,10},{9,11},{10,... | collective-permute-start | bytes 405512 | tf_op jit(solution)/shard_map/ppermute | solution.py:200
  12.9 1.5 %collective-permute-start.3 = (bf16[528,128]{1,0:T(8,128)(2,1)S(1)}, bf16[528,128]{1,0:T(8,128)(2,1)S(1)}, u32[]{:S(2)}, u32[]{:S(2)}) collective-permute-start(bf16[528,128]{1,0:T(8,128)(2,1)S(1)} %collective-permute-done.2.refs_4_), channel_id=1, source_target_pairs={{0,4},{1,5},{2,6},{3,7},{4,0},{5,1},{6,2},{7,3},{8,12},{9,13},{10,... | collective-permute-start | bytes 405512 | tf_op jit(solution)/shard_map/ppermute | solution.py:200
  14.4 0.0 collective-permute-done.1.refs_3_
  14.4 0.5 %collective-permute-start.4 = (bf16[528,128]{1,0:T(8,128)(2,1)S(1)}, bf16[528,128]{1,0:T(8,128)(2,1)S(1)}, u32[]{:S(2)}, u32[]{:S(2)}) collective-permute-start(bf16[528,128]{1,0:T(8,128)(2,1)S(1)} %collective-permute-done.1.refs_3_), channel_id=1, source_target_pairs={{0,2},{1,3},{2,0},{3,1},{4,6},{5,7},{6,4},{7,5},{8,10},{9,11},{10,... | collective-permute-start | bytes 405512 | tf_op jit(solution)/shard_map/ppermute | solution.py:200
  14.9 0.0 collective-permute-done.refs_2_
  14.9 1.5 %collective-permute-start.6 = (bf16[528,128]{1,0:T(8,128)(2,1)S(1)}, bf16[528,128]{1,0:T(8,128)(2,1)S(1)}, u32[]{:S(2)}, u32[]{:S(2)}) collective-permute-start(bf16[528,128]{1,0:T(8,128)(2,1)S(1)} %collective-permute-done.2.refs_4_), channel_id=1, source_target_pairs={{0,6},{1,7},{2,4},{3,5},{4,2},{5,3},{6,0},{7,1},{8,14},{9,15},{10,... | collective-permute-start | bytes 405512 | tf_op jit(solution)/shard_map/ppermute | solution.py:200
  16.4 0.0 collective-permute-done.7.refs_0_
  16.4 0.0 collective-permute-done.5.refs_7_.refs_5_.refs_3_
  16.4 1.0 %absorb_theirs.2 = (f32[128,1024]{1,0:T(8,128)S(1)}, f32[2,1024]{1,0:T(2,128)S(1)}) custom-call(bf16[1040,128]{1,0:T(8,128)(2,1)S(1)} %collective-permute-done.7.refs_0_, bf16[528,128]{1,0:T(8,128)(2,1)S(1)} %pack_keys_values.1.message_ref.refs_1_, bf16[528,128]{1,0:T(8,128)(2,1)S(1)} %collective-permute-done.refs_2_, ...), custom_call_target="tpu_custom_call" | custom-call | flops 268435456 | bytes 1048576 | tf_op jit(solution)/shard_map/absorb_theirs/pallas_call | solution.py:209
  17.5 1.3 %collective-permute-done.3.refs_5_ = bf16[528,128]{1,0:T(8,128)(2,1)S(1)} collective-permute-done((bf16[528,128]{1,0:T(8,128)(2,1)S(1)}, bf16[528,128]{1,0:T(8,128)(2,1)S(1)}, u32[]{:S(2)}, u32[]{:S(2)}) %collective-permute-start.3) | collective-permute-done | bytes 135200 | tf_op jit(solution)/shard_map/ppermute | solution.py:200
  18.8 0.7 %collective-permute-done.4.refs_6_.refs_4_ = bf16[528,128]{1,0:T(8,128)(2,1)S(1)} collective-permute-done((bf16[528,128]{1,0:T(8,128)(2,1)S(1)}, bf16[528,128]{1,0:T(8,128)(2,1)S(1)}, u32[]{:S(2)}, u32[]{:S(2)}) %collective-permute-start.4) | collective-permute-done | bytes 135200 | tf_op jit(solution)/shard_map/ppermute | solution.py:200
  19.4 0.9 %absorb_theirs.3 = (f32[128,1024]{1,0:T(8,128)S(1)}, f32[2,1024]{1,0:T(2,128)S(1)}) custom-call(bf16[1040,128]{1,0:T(8,128)(2,1)S(1)} %collective-permute-done.7.refs_0_, f32[128,1024]{1,0:T(8,128)S(1)} %get-tuple-element.10.refs_1_, f32[2,1024]{1,0:T(2,128)S(1)} %get-tuple-element.11.refs_2_, ...), custom_call_target="tpu_custom_call" | custom-call | flops 201326592 | bytes 1048576 | tf_op jit(solution)/shard_map/absorb_theirs/pallas_call | solution.py:209
  20.3 0.6 %collective-permute-done.6.refs_8_.refs_3_ = bf16[528,128]{1,0:T(8,128)(2,1)S(1)} collective-permute-done((bf16[528,128]{1,0:T(8,128)(2,1)S(1)}, bf16[528,128]{1,0:T(8,128)(2,1)S(1)}, u32[]{:S(2)}, u32[]{:S(2)}) %collective-permute-start.6) | collective-permute-done | bytes 135200 | tf_op jit(solution)/shard_map/ppermute | solution.py:200
  20.9 0.5 %message.1 = bf16[1056,128]{1,0:T(8,128)(2,1)S(1)} custom-call(bf16[1040,128]{1,0:T(8,128)(2,1)S(1)} %collective-permute-done.7.refs_0_, f32[128,1024]{1,0:T(8,128)S(1)} %get-tuple-element.12.refs_1_, f32[2,1024]{1,0:T(2,128)S(1)} %get-tuple-element.13.refs_2_, bf16[528,128]{1,0:T(8,128)(2,1)S(1)} %collective-permute-done.6.refs_8_.refs_3_), custom_call_target="tpu_custom_call" | custom-call | flops 67108864 | bytes 1048576 | tf_op jit(solution)/shard_map/message/pallas_call | solution.py:239
  21.3 1.6 %collective-permute-start.8 = (bf16[1056,128]{1,0:T(8,128)(2,1)S(1)}, bf16[1056,128]{1,0:T(8,128)(2,1)S(1)}, u32[]{:S(2)}, u32[]{:S(2)}) collective-permute-start(bf16[1056,128]{1,0:T(8,128)(2,1)S(1)} %message.1), channel_id=1, source_target_pairs={{0,1},{1,0},{2,3},{3,2},{4,5},{5,4},{6,7},{7,6},{8,9},{9,8},{10,11... | collective-permute-start | bytes 811016 | tf_op jit(solution)/shard_map/ppermute | solution.py:200
  22.9 2.2 %absorb_mine.1 = (f32[128,1024]{1,0:T(8,128)S(1)}, f32[2,1024]{1,0:T(2,128)S(1)}) custom-call(bf16[1040,128]{1,0:T(8,128)(2,1)S(1)} %pack_queries.1.refs_0_, bf16[528,128]{1,0:T(8,128)(2,1)S(1)} %pack_keys_values.1.message_ref.refs_1_, bf16[528,128]{1,0:T(8,128)(2,1)S(1)} %collective-permute-done.refs_2_, ...), custom_call_target="tpu_custom_call" | custom-call | flops 536870912 | bytes 1048576 | tf_op jit(solution)/shard_map/absorb_mine/pallas_call | solution.py:209
  25.1 2.7 %collective-permute-done.8.message_ref = bf16[1056,128]{1,0:T(8,128)(2,1)S(1)} collective-permute-done((bf16[1056,128]{1,0:T(8,128)(2,1)S(1)}, bf16[1056,128]{1,0:T(8,128)(2,1)S(1)}, u32[]{:S(2)}, u32[]{:S(2)}) %collective-permute-start.8) | collective-permute-done | bytes 270368 | tf_op jit(solution)/shard_map/ppermute | solution.py:200
  27.8 0.9 %finish.1 = (bf16[128,1024]{1,0:T(8,128)(2,1)}, f32[8,128]{1,0:T(8,128)}) custom-call(f32[128,1024]{1,0:T(8,128)S(1)} %get-tuple-element.8.acc_ref, f32[2,1024]{1,0:T(2,128)S(1)} %get-tuple-element.9.stat_ref, bf16[1056,128]{1,0:T(8,128)(2,1)S(1)} %collective-permute-done.8.message_ref), custom_call_target="tpu_custom_call" | custom-call | bytes 1048576 | tf_op jit(solution)/shard_map/finish/pallas_call | solution.py:251
Async XLA Ops:
  0.6 6.0 %copy-start = (bf16[128,1024]{1,0:T(8,128)(2,1)S(1)}, bf16[128,1024]{1,0:T(8,128)(2,1)}, u32[]{:S(2)}) copy-start(bf16[128,1024]{1,0:T(8,128)(2,1)} %queries_ref.1) | copy-start | bytes 786436
  1.6 9.6 %collective-permute-start.2 = (bf16[528,128]{1,0:T(8,128)(2,1)S(1)}, bf16[528,128]{1,0:T(8,128)(2,1)S(1)}, u32[]{:S(2)}, u32[]{:S(2)}) collective-permute-start(bf16[528,128]{1,0:T(8,128)(2,1)S(1)} %pack_keys_values.1.message_ref.refs_1_), channel_id=1, source_target_pairs={{0,12},{1,13},{2,14},{3,15},{4,8},{5,9},{6,10},{7,11},{8,4},{9,5},... | collective-permute-start | bytes 405512 | tf_op jit(solution)/shard_map/ppermute | solution.py:200
  6.8 9.6 %collective-permute-start.7 = (bf16[1040,128]{1,0:T(8,128)(2,1)S(1)}, bf16[1040,128]{1,0:T(8,128)(2,1)S(1)}, u32[]{:S(2)}, u32[]{:S(2)}) collective-permute-start(bf16[1040,128]{1,0:T(8,128)(2,1)S(1)} %pack_queries.1.refs_0_), channel_id=1, source_target_pairs={{0,1},{1,0},{2,3},{3,2},{4,5},{5,4},{6,7},{7,6},{8,9},{9,8},{10,11... | collective-permute-start | bytes 798728 | tf_op jit(solution)/shard_map/ppermute | solution.py:200
  8.4 6.0 %collective-permute-start.1 = (bf16[528,128]{1,0:T(8,128)(2,1)S(1)}, bf16[528,128]{1,0:T(8,128)(2,1)S(1)}, u32[]{:S(2)}, u32[]{:S(2)}) collective-permute-start(bf16[528,128]{1,0:T(8,128)(2,1)S(1)} %pack_keys_values.1.message_ref.refs_1_), channel_id=1, source_target_pairs={{0,4},{1,5},{2,6},{3,7},{4,0},{5,1},{6,2},{7,3},{8,12},{9,13},{10,... | collective-permute-start | bytes 405512 | tf_op jit(solution)/shard_map/ppermute | solution.py:200
  8.4 6.5 %collective-permute-start = (bf16[528,128]{1,0:T(8,128)(2,1)S(1)}, bf16[528,128]{1,0:T(8,128)(2,1)S(1)}, u32[]{:S(2)}, u32[]{:S(2)}) collective-permute-start(bf16[528,128]{1,0:T(8,128)(2,1)S(1)} %pack_keys_values.1.message_ref.refs_1_), channel_id=1, source_target_pairs={{0,2},{1,3},{2,0},{3,1},{4,6},{5,7},{6,4},{7,5},{8,10},{9,11},{10,... | collective-permute-start | bytes 405512 | tf_op jit(solution)/shard_map/ppermute | solution.py:200
  11.1 5.3 %collective-permute-start.5 = (bf16[528,128]{1,0:T(8,128)(2,1)S(1)}, bf16[528,128]{1,0:T(8,128)(2,1)S(1)}, u32[]{:S(2)}, u32[]{:S(2)}) collective-permute-start(bf16[528,128]{1,0:T(8,128)(2,1)S(1)} %collective-permute-done.2.refs_4_), channel_id=1, source_target_pairs={{0,2},{1,3},{2,0},{3,1},{4,6},{5,7},{6,4},{7,5},{8,10},{9,11},{10,... | collective-permute-start | bytes 405512 | tf_op jit(solution)/shard_map/ppermute | solution.py:200
  12.9 5.9 %collective-permute-start.3 = (bf16[528,128]{1,0:T(8,128)(2,1)S(1)}, bf16[528,128]{1,0:T(8,128)(2,1)S(1)}, u32[]{:S(2)}, u32[]{:S(2)}) collective-permute-start(bf16[528,128]{1,0:T(8,128)(2,1)S(1)} %collective-permute-done.2.refs_4_), channel_id=1, source_target_pairs={{0,4},{1,5},{2,6},{3,7},{4,0},{5,1},{6,2},{7,3},{8,12},{9,13},{10,... | collective-permute-start | bytes 405512 | tf_op jit(solution)/shard_map/ppermute | solution.py:200
  14.4 5.0 %collective-permute-start.4 = (bf16[528,128]{1,0:T(8,128)(2,1)S(1)}, bf16[528,128]{1,0:T(8,128)(2,1)S(1)}, u32[]{:S(2)}, u32[]{:S(2)}) collective-permute-start(bf16[528,128]{1,0:T(8,128)(2,1)S(1)} %collective-permute-done.1.refs_3_), channel_id=1, source_target_pairs={{0,2},{1,3},{2,0},{3,1},{4,6},{5,7},{6,4},{7,5},{8,10},{9,11},{10,... | collective-permute-start | bytes 405512 | tf_op jit(solution)/shard_map/ppermute | solution.py:200
  14.9 6.0 %collective-permute-start.6 = (bf16[528,128]{1,0:T(8,128)(2,1)S(1)}, bf16[528,128]{1,0:T(8,128)(2,1)S(1)}, u32[]{:S(2)}, u32[]{:S(2)}) collective-permute-start(bf16[528,128]{1,0:T(8,128)(2,1)S(1)} %collective-permute-done.2.refs_4_), channel_id=1, source_target_pairs={{0,6},{1,7},{2,4},{3,5},{4,2},{5,3},{6,0},{7,1},{8,14},{9,15},{10,... | collective-permute-start | bytes 405512 | tf_op jit(solution)/shard_map/ppermute | solution.py:200
  21.3 6.5 %collective-permute-start.8 = (bf16[1056,128]{1,0:T(8,128)(2,1)S(1)}, bf16[1056,128]{1,0:T(8,128)(2,1)S(1)}, u32[]{:S(2)}, u32[]{:S(2)}) collective-permute-start(bf16[1056,128]{1,0:T(8,128)(2,1)S(1)} %message.1), channel_id=1, source_target_pairs={{0,1},{1,0},{2,3},{3,2},{4,5},{5,4},{6,7},{7,6},{8,9},{9,8},{10,11... | collective-permute-start | bytes 811016 | tf_op jit(solution)/shard_map/ppermute | solution.py:200
